TPU v7x, 512 devices: a whole 4x8x8 slice. The times are simulated.
512 devices in a mesh: seq: 16 (over z, core), batch: 32 (over x, y).
Axes of the slice: x: 4, y: 8, z: 8, core: 2. Of those that a mesh axis runs over, the one named last changes fastest.
Arguments:
- queries: bfloat16 [65536, 4096], P(('batch', 'seq')), parts along dimension 0, may hold values from -12 to 12
- key_vectors: bfloat16 [65536, 4096], P(('batch', 'seq')), parts along dimension 0, may hold values from -12 to 12
- value_vectors: bfloat16 [65536, 4096], P(('batch', 'seq')), parts along dimension 0, may hold values from -6 to 6
- keep_list: int32 [1024, 96], P(('batch', 'seq')), parts along dimension 0, may hold values from 0 to 254, as said below
- block_counts: int32 [1024], P('batch'), parts along dimension 0, may hold values from 1 to 96, as said below
Outputs:
- attended: bfloat16 [65536, 4096], P(('batch', 'seq')), parts along dimension 0
There are 32 independent parts, one for each index of `batch`. A program takes and returns all parts, laid end to end along the dimension named above; each array names one. Nothing has to cross between parts.
Inputs may be any that keep to these rules, and one draw needn't show every extreme that they name: `keep_list`: row h holds 96 distinct cells a * 16 + b of head h's block grid, never one with a == b. Head h keeps the first block_counts[h] cells of its keep list; one head has 96 and one has 1.
All inputs are finite; a program needn't handle non-finite values.
Results may differ from a plain program's by a relative error of at most 0.0027.
Values may be sent and summed in bfloat16 or wider, within the bound.
No kernel may reach another device: no remote copies, remote signals or barrier semaphores. Data moves between devices by JAX's collectives and lax.ppermute only.
A program may use at most 64 MiB of HBM per device.

v0:
```python
import jax
import jax.numpy as jnp
from jax import lax
from jax.sharding import PartitionSpec as P

BLK = 128


neg_large = -1e30
group_size = 32


def tile_partials(query_tiles, key_tiles, value_tiles, score_scale):
    scores = (
        jnp.einsum("gid,gjd->gij", query_tiles, key_tiles, preferred_element_type=jnp.float32)
        * score_scale
    )
    maxima = jnp.max(scores, axis=2)
    weights = jnp.exp(scores - maxima[:, :, None])
    totals = jnp.sum(weights, axis=2)
    outputs = jnp.einsum(
        "gij,gjd->gid",
        weights.astype(jnp.bfloat16),
        value_tiles,
        preferred_element_type=jnp.float32,
    )
    return (outputs, maxima, totals)


def merge_tiles(states, outputs, maxima, totals, slot_ids, is_valid):
    old_max, old_total, old_acc = states
    slot_count = old_max.shape[0]
    maxima = jnp.where(is_valid[:, None], maxima, neg_large)
    onehot = (slot_ids[:, None] == jnp.arange(slot_count)[None, :]) & is_valid[:, None]
    candidate = jnp.max(jnp.where(onehot[:, :, None], maxima[:, None, :], neg_large), axis=0)
    new_max = jnp.maximum(old_max, candidate)
    rescale = jnp.exp(old_max - new_max)
    factor = jnp.exp(maxima - new_max[jnp.where(is_valid, slot_ids, 0)])
    indicator = onehot.astype(jnp.float32)
    new_total = old_total * rescale + jnp.einsum(
        "gs,gi->si", indicator, factor * totals, precision=lax.Precision.HIGHEST
    )
    scaled = jnp.where(is_valid[:, None, None], factor[:, :, None] * outputs, 0.0)
    new_acc = old_acc * rescale[:, :, None] + jnp.einsum(
        "gs,gid->sid", indicator, scaled, precision=lax.Precision.HIGHEST
    )
    return (new_max, new_total, new_acc)


def on_device(queries, key_vectors, value_vectors, keep_list, block_counts):
    peer_count = lax.axis_size("seq")
    my_index = lax.axis_index("seq")
    head_total = block_counts.shape[0]
    heads_here = head_total // peer_count
    head_dim = queries.shape[1] // head_total
    tok_local = queries.shape[0]
    length = tok_local * peer_count
    block_rows = BLK
    nblocks = length // block_rows
    list_len = keep_list.shape[1]
    score_scale = head_dim ** (-0.5)
    query_heads = queries.reshape(tok_local, head_total, head_dim)
    key_heads = key_vectors.reshape(tok_local, head_total, head_dim)
    value_heads = value_vectors.reshape(tok_local, head_total, head_dim)
    owners = jnp.arange(peer_count)[:, None] * heads_here + jnp.arange(heads_here)[None, :]
    my_heads = owners[my_index]
    my_counts = block_counts[my_heads]
    arrived_heads = (
        lax.all_to_all(query_heads, "seq", split_axis=1, concat_axis=0, tiled=True),
        lax.all_to_all(key_heads, "seq", split_axis=1, concat_axis=0, tiled=True),
        lax.all_to_all(value_heads, "seq", split_axis=1, concat_axis=0, tiled=True),
    )
    query_tiles = arrived_heads[0].reshape(nblocks, block_rows, heads_here, head_dim)
    key_tiles = arrived_heads[1].reshape(nblocks, block_rows, heads_here, head_dim)
    value_tiles = arrived_heads[2].reshape(nblocks, block_rows, heads_here, head_dim)
    slot_count = nblocks * heads_here
    scores = (
        jnp.einsum("bihd,bjhd->bhij", query_tiles, key_tiles, preferred_element_type=jnp.float32)
        * score_scale
    )
    maxima = jnp.max(scores, axis=3)
    weights = jnp.exp(scores - maxima[..., None])
    totals = jnp.sum(weights, axis=3)
    outputs = jnp.einsum(
        "bhij,bjhd->bhid",
        weights.astype(jnp.bfloat16),
        value_tiles,
        preferred_element_type=jnp.float32,
    )
    states = (
        maxima.reshape(slot_count, block_rows),
        totals.reshape(slot_count, block_rows),
        outputs.reshape(slot_count, block_rows, head_dim),
    )
    starts = jnp.cumsum(my_counts) - my_counts
    my_load = jnp.sum(my_counts)

    def locate(item_ids):
        head_pos = jnp.sum(item_ids[:, None] >= starts[None, :], axis=1) - 1
        offset = jnp.clip(item_ids - starts[head_pos], 0, list_len - 1)
        flat_cell = keep_list[head_pos, offset]
        row_block = flat_cell // nblocks
        col_block = flat_cell % nblocks
        return (head_pos, row_block, col_block, row_block * heads_here + head_pos)

    def fetch_tiles(head_pos, row_block, col_block):
        return (
            query_tiles[row_block, :, head_pos, :],
            key_tiles[col_block, :, head_pos, :],
            value_tiles[col_block, :, head_pos, :],
        )

    def one_group(group_index, carried):
        item_ids = group_index * group_size + jnp.arange(group_size)
        is_valid = item_ids < my_load
        head_pos, row_block, col_block, slot_ids = locate(jnp.where(is_valid, item_ids, 0))
        partial_value = tile_partials(*fetch_tiles(head_pos, row_block, col_block), score_scale)
        return merge_tiles(
            carried, partial_value[0], partial_value[1], partial_value[2], slot_ids, is_valid
        )

    states = lax.fori_loop(0, (my_load + group_size - 1) // group_size, one_group, states)
    best_max, best_total, accumulated = states
    result = accumulated / best_total[:, :, None]
    result = result.reshape(nblocks, heads_here, block_rows, head_dim).transpose(0, 2, 1, 3)
    result = result.reshape(length, heads_here, head_dim).astype(jnp.bfloat16)
    returned_heads = lax.all_to_all(result, "seq", split_axis=0, concat_axis=1, tiled=True)
    return returned_heads.reshape(tok_local, head_total * head_dim)


def solution(mesh):
    placed = (
        P(("batch", "seq"), None),
        P(("batch", "seq"), None),
        P(("batch", "seq"), None),
        P(("batch", "seq"), None),
        P("batch"),
    )
    return jax.shard_map(
        on_device, mesh=mesh, in_specs=placed, out_specs=P(("batch", "seq"), None), check_vma=False
    )
```

profile of v0, /device:TPU:55, one launch (start us, length us, event | category | flops | bytes accessed | tf_op | source)
XLA Modules:
  0.0 321.3 jit_solution(1754009452830281030)
XLA Ops:
  0.0 1.2 copy-done
  1.2 1.3 copy_bitcast_fusion.2
  2.5 11.0 %all-to-all-start = ((bf16[128,32,128]{2,0,1:T(8,128)(2,1)}), bf16[128,32,128]{2,0,1:T(8,128)(2,1)S(1)}, u32[]{:S(2)}, u32[]{:S(2)}) async-start(bf16[128,32,128]{2,0,1:T(8,128)(2,1)} %copy_bitcast_fusion.2), calls=%async_computation | async-start | bytes 2097152 | tf_op jit(solution)/shard_map/all_to_all | solution.py:69
  13.5 1.3 copy_bitcast_fusion.1
  14.8 26.6 %all-to-all-done = bf16[128,32,128]{2,0,1:T(8,128)(2,1)S(1)} async-done(((bf16[128,32,128]{2,0,1:T(8,128)(2,1)}), bf16[128,32,128]{2,0,1:T(8,128)(2,1)S(1)}, u32[]{:S(2)}, u32[]{:S(2)}) %all-to-all-start) | async-done | bytes 1048608 | tf_op jit(solution)/shard_map/all_to_all | solution.py:69
  41.4 3.6 %all-to-all-start.1 = ((bf16[128,32,128]{2,0,1:T(8,128)(2,1)}), bf16[128,32,128]{2,0,1:T(8,128)(2,1)S(1)}, u32[]{:S(2)}, u32[]{:S(2)}) async-start(bf16[128,32,128]{2,0,1:T(8,128)(2,1)} %copy_bitcast_fusion.1), calls=%async_computation.1 | async-start | bytes 2097152 | tf_op jit(solution)/shard_map/all_to_all | solution.py:70
  45.0 2.5 copy_bitcast_fusion
  47.5 25.4 %all-to-all-done.1 = bf16[128,32,128]{2,0,1:T(8,128)(2,1)S(1)} async-done(((bf16[128,32,128]{2,0,1:T(8,128)(2,1)}), bf16[128,32,128]{2,0,1:T(8,128)(2,1)S(1)}, u32[]{:S(2)}, u32[]{:S(2)}) %all-to-all-start.1) | async-done | bytes 1048608 | tf_op jit(solution)/shard_map/all_to_all | solution.py:70
  72.9 1.0 copy-done.7
  73.9 3.5 %all-to-all-start.2 = ((bf16[128,32,128]{2,0,1:T(8,128)(2,1)}), bf16[128,32,128]{2,0,1:T(8,128)(2,1)S(1)}, u32[]{:S(2)}, u32[]{:S(2)}) async-start(bf16[128,32,128]{2,0,1:T(8,128)(2,1)} %copy_bitcast_fusion), calls=%async_computation.2 | async-start | bytes 2097152 | tf_op jit(solution)/shard_map/all_to_all | solution.py:71
  78.1 0.7 fusion.39
  79.6 0.7 bitcast_subtract_fusion
  81.1 2.1 multiply_reduce_fusion.1
  83.2 1.3 copy-done.8
  85.0 20.4 %all-to-all-done.2 = bf16[128,32,128]{2,0,1:T(8,128)(2,1)S(1)} async-done(((bf16[128,32,128]{2,0,1:T(8,128)(2,1)}), bf16[128,32,128]{2,0,1:T(8,128)(2,1)S(1)}, u32[]{:S(2)}, u32[]{:S(2)}) %all-to-all-start.2) | async-done | bytes 1048608 | tf_op jit(solution)/shard_map/all_to_all | solution.py:71
  105.3 2.2 fusion.35
  107.5 2.5 copy.65
  110.0 28.0 %while.19 = (s32[]{:T(128)}, f32[32,128]{1,0:T(8,128)S(1)}, f32[32,128]{1,0:T(8,128)S(1)}, f32[32,128,128]{2,0,1:T(8,128)}, s32[]{:T(128)}, /*index=5*/s32[]{:T(...) while((s32[]{:T(128)}, f32[32,128]{1,0:T(8,128)S(1)}, ...), condition=%wide.region_9.10_spmd, body=%wide.region_4.9_spmd.sunk | while | flops 477919104 | bytes 41332768 | solution.py:122
  111.4 1.9 fusion.79
  113.3 0.8 gather_fusion
  114.1 0.7 fusion.80
  114.8 1.7 gather_fusion.1
  116.5 2.9 gather_fusion.2
  119.4 2.4 multiply_reduce_fusion.3
  121.8 0.7 fusion.81
  124.2 2.9 gather_fusion.4
  127.1 3.7 %multiply_select_fusion.2 = f32[32,128,128]{2,1,0:T(8,128)} fusion(bf16[32,128,128]{2,1,0:T(8,128)(2,1)} %gather_fusion.4, f32[32,128,128]{1,2,0:T(8,128)S(1)} %get-tuple-element.442, f32[32,128]{1,0:T(8,128)S(1)} %subtract_exponential_fusion.7, f32[32,128]{1,0:T(8,128)S(1)} %get-tuple-element.439, pred[32]{0:T(512)(128)(4,1)S(1)} %fusion.81), kind=kOutput, calls=%fused_computation.8.clone.1 | convolution fusion | flops 136839168 | bytes 5275680 | tf_op jit(solution)/shard_map/while/body/gij,gjd->gid/dot_general | solution.py:21
  130.9 7.1 %multiply_add_fusion.5 = f32[32,128,128]{2,0,1:T(8,128)} fusion(f32[32,128,128]{2,0,1:T(8,128)} %get-tuple-element.460, f32[32,128,128]{2,1,0:T(8,128)} %multiply_select_fusion.2, f32[32,128]{0,1:T(8,128)S(1)} %copy.92, s32[32]{0:T(128)S(1)} %multiply_add_fusion.4, pred[32]{0:T(512)(128)(4,1)S(1)} %fusion.81), kind=kOutput, calls=%fused_computation.9.clone.1 | convolution fusion | flops 202377216 | bytes 6308000 | tf_op jit(solution)/shard_map/while/body/gs,gid->sid/dot_general | solution.py:44
  138.0 2.5 fusion.32
  140.6 8.7 %copy.68 = bf16[2048,2,128]{2,1,0:T(2,128)(2,1)S(1)} copy(bf16[2048,2,128]{2,0,1:T(8,128)(2,1)S(1)} %bitcast.136) | data formatting | bytes 2097152 | tf_op jit(solution)/shard_map/convert_element_type | solution.py:126
  149.3 169.9 %all_to_all.60 = bf16[2048,2,128]{2,1,0:T(2,128)(2,1)S(1)} all-to-all(bf16[2048,2,128]{2,1,0:T(2,128)(2,1)S(1)} %copy.68), channel_id=1, replica_groups=mesh['seq'=16,'batch'=32] {'seq'}, dimensions={0} | all-to-all | bytes 2097152 | tf_op jit(solution)/shard_map/all_to_all | solution.py:127
  320.0 1.3 copy.71
  (41 shorter events, 5.9 us)
Async XLA Ops:
  0.0 1.2 copy-start
  0.0 13.5 %copy-start.9 = (bf16[128,4096]{1,0:T(8,128)(2,1)S(1)}, bf16[128,4096]{1,0:T(8,128)(2,1)}, u32[]{:S(2)}) copy-start(bf16[128,4096]{1,0:T(8,128)(2,1)} %param.8) | copy-start | bytes 3145732
  2.5 38.9 %all-to-all-start = ((bf16[128,32,128]{2,0,1:T(8,128)(2,1)}), bf16[128,32,128]{2,0,1:T(8,128)(2,1)S(1)}, u32[]{:S(2)}, u32[]{:S(2)}) async-start(bf16[128,32,128]{2,0,1:T(8,128)(2,1)} %copy_bitcast_fusion.2), calls=%async_computation | async-start | bytes 2097152 | tf_op jit(solution)/shard_map/all_to_all | solution.py:69
  41.4 31.5 %all-to-all-start.1 = ((bf16[128,32,128]{2,0,1:T(8,128)(2,1)}), bf16[128,32,128]{2,0,1:T(8,128)(2,1)S(1)}, u32[]{:S(2)}, u32[]{:S(2)}) async-start(bf16[128,32,128]{2,0,1:T(8,128)(2,1)} %copy_bitcast_fusion.1), calls=%async_computation.1 | async-start | bytes 2097152 | tf_op jit(solution)/shard_map/all_to_all | solution.py:70
  45.0 33.8 %copy-start.2 = (s32[32]{0:T(128)S(1)}, s32[32]{0:T(128)}, u32[]{:S(2)}) copy-start(s32[32]{0:T(128)} %param.11) | copy-start | bytes 388
  72.9 1.0 copy-start.7
  73.9 31.5 %all-to-all-start.2 = ((bf16[128,32,128]{2,0,1:T(8,128)(2,1)}), bf16[128,32,128]{2,0,1:T(8,128)(2,1)S(1)}, u32[]{:S(2)}, u32[]{:S(2)}) async-start(bf16[128,32,128]{2,0,1:T(8,128)(2,1)} %copy_bitcast_fusion), calls=%async_computation.2 | async-start | bytes 2097152 | tf_op jit(solution)/shard_map/all_to_all | solution.py:71
  83.2 1.4 copy-start.8
  107.5 2.5 copy-start.1
  110.0 6.5 %copy-start.3 = (bf16[16,128,2,128]{3,1,2,0:T(8,128)(2,1)}, bf16[16,128,2,128]{3,1,2,0:T(8,128)(2,1)S(1)}, u32[]{:S(2)}) copy-start(bf16[16,128,2,128]{3,1,2,0:T(8,128)(2,1)S(1)} %get-tuple-element.480) | copy-start | bytes 3145732 | tf_op jit(solution)/shard_map/while
  110.0 6.5 %copy-start.5 = (bf16[16,128,2,128]{3,1,2,0:T(8,128)(2,1)}, bf16[16,128,2,128]{3,1,2,0:T(8,128)(2,1)S(1)}, u32[]{:S(2)}) copy-start(bf16[16,128,2,128]{3,1,2,0:T(8,128)(2,1)S(1)} %get-tuple-element.478) | copy-start | bytes 3145732 | tf_op jit(solution)/shard_map/while
  130.9 7.2 %copy-start.4 = (bf16[16,128,2,128]{3,1,2,0:T(8,128)(2,1)S(1)}, bf16[16,128,2,128]{3,1,2,0:T(8,128)(2,1)}, u32[]{:S(2)}) copy-start(bf16[16,128,2,128]{3,1,2,0:T(8,128)(2,1)} %copy-done.3) | copy-start | bytes 3145732 | tf_op jit(solution)/shard_map/while
  130.9 7.1 %copy-start.6 = (bf16[16,128,2,128]{3,1,2,0:T(8,128)(2,1)S(1)}, bf16[16,128,2,128]{3,1,2,0:T(8,128)(2,1)}, u32[]{:S(2)}) copy-start(bf16[16,128,2,128]{3,1,2,0:T(8,128)(2,1)} %copy-done.5) | copy-start | bytes 3145732 | tf_op jit(solution)/shard_map/while
where the time goes:
time: 326 us; the launch traced here: 321 us
  blocking collectives  170 us (52%)
  waiting for transfers between devices  72.4 us (22%)
  local copies, waits for them, and re-layouts  33 us (10%)
  starting transfers between devices  18.1 us (6%)
  matrix products  17.6 us (5%)
  other arithmetic  9.39 us (3%)
    all_to_all x1, blocking collectives, on_device(): lax.all_to_all(result, 'seq', split_axis=0, concat_axis=1, tiled=True)  170 us
    all_to_all x1, waiting for transfers between devices, on_device(): lax.all_to_all(query_heads, 'seq', split_axis=1, concat_axis=0, tiled=True)  26.6 us
    all_to_all x1, waiting for transfers between devices, on_device(): lax.all_to_all(key_heads, 'seq', split_axis=1, concat_axis=0, tiled=True)  25.4 us
    all_to_all x1, waiting for transfers between devices, on_device(): lax.all_to_all(value_heads, 'seq', split_axis=1, concat_axis=0, tiled=True)  20.4 us
    all_to_all x1, starting transfers between devices, on_device(): lax.all_to_all(query_heads, 'seq', split_axis=1, concat_axis=0, tiled=True)  11 us
    convert_element_type x2, local copies, waits for them, and re-layouts, on_device(): result = result.reshape(length, heads_here, head_dim).astype(jnp.bfloat16)  8.78 us
    dot_general x1, matrix products, merge_tiles(): jnp.einsum('gs,gid->sid', indicator, scaled, precision=lax.Precision.HIGH...  7.13 us
  transfers between devices with their start and end apart: 3, of which 3 were waited for; matrix products, arithmetic and copies ran while one was open for 3% of the time, Pallas kernels for 0%

commit v1 on v0

v1 whole, which is shorter than its diff:
```python
import functools
import math

import jax
import jax.numpy as jnp
from jax import lax
from jax.experimental import pallas as pl
from jax.experimental.pallas import tpu as pltpu
from jax.sharding import PartitionSpec as P

BLK = 128
GROUP = 4
neg_large = -1e30


def cell_partial(keys, queries, values_t, factor):
    scores = lax.dot_general(
        keys, queries, (((1,), (1,)), ((), ())), preferred_element_type=jnp.float32
    )
    scores = scores * factor
    block_max = jnp.max(scores, axis=0, keepdims=True)
    weights = jnp.exp2(scores - block_max)
    block_total = jnp.sum(weights, axis=0, keepdims=True)
    block_out = lax.dot_general(
        values_t,
        weights.astype(jnp.bfloat16),
        (((1,), (0,)), ((), ())),
        preferred_element_type=jnp.float32,
    )
    return block_max, block_total, block_out


def head_kernel(factor, cells, count, tiles, out, acc, row_max, row_total):
    nblocks = tiles.shape[0]
    live = count[0]

    for row in range(0, nblocks, GROUP):
        for a in range(row, row + GROUP):
            block_max, block_total, block_out = cell_partial(
                tiles[a, 1], tiles[a, 0], tiles[a, 2], factor
            )
            acc[a] = block_out
            row_max[a] = block_max
            row_total[a] = block_total

    def step(index, carry):
        partials = []
        for slot in range(GROUP):
            entry = index * GROUP + slot
            cell = cells[jnp.minimum(entry, live - 1)]
            a = lax.shift_right_logical(cell, 4)
            b = lax.bitwise_and(cell, 15)
            block_max, block_total, block_out = cell_partial(
                tiles[b, 1], tiles[a, 0], tiles[b, 2], factor
            )
            block_max = jnp.where(entry < live, block_max, neg_large)
            partials.append((a, block_max, block_total, block_out))
        for a, block_max, block_total, block_out in partials:
            old_max = row_max[a]
            new_max = jnp.maximum(old_max, block_max)
            rescale = jnp.exp2(old_max - new_max)
            share = jnp.exp2(block_max - new_max)
            row_max[a] = new_max
            row_total[a] = row_total[a] * rescale + block_total * share
            acc[a] = acc[a] * rescale + block_out * share
        return carry

    lax.fori_loop(0, (live + GROUP - 1) // GROUP, step, 0)

    for a in range(nblocks):
        out[a] = (acc[a] / row_total[a]).T.astype(out.dtype)


def attend(tiles, cells, count, name):
    nblocks, _, rows, head_dim = tiles.shape
    factor = head_dim ** (-0.5) * math.log2(math.e)
    vmem = pl.BlockSpec(memory_space=pltpu.VMEM)
    smem = pl.BlockSpec(memory_space=pltpu.SMEM)
    return pl.pallas_call(
        functools.partial(head_kernel, factor),
        out_shape=jax.ShapeDtypeStruct((nblocks, rows, head_dim), jnp.bfloat16),
        in_specs=[smem, smem, vmem],
        out_specs=vmem,
        scratch_shapes=[
            pltpu.VMEM((nblocks, head_dim, rows), jnp.float32),
            pltpu.VMEM((nblocks, 1, rows), jnp.float32),
            pltpu.VMEM((nblocks, 1, rows), jnp.float32),
        ],
        compiler_params=pltpu.CompilerParams(vmem_limit_bytes=16 * 1024 * 1024),
        cost_estimate=pl.CostEstimate(
            flops=4 * 64 * rows * rows * head_dim,
            bytes_accessed=2 * 4 * nblocks * rows * head_dim,
            transcendentals=64 * rows * rows,
        ),
        name=name,
    )(cells, count, tiles)


def on_device(queries, key_vectors, value_vectors, keep_list, block_counts):
    peers = lax.axis_size("seq")
    me = lax.axis_index("seq")
    head_total = block_counts.shape[0]
    heads_here = head_total // peers
    head_dim = queries.shape[1] // head_total
    tok_local = queries.shape[0]
    split = (tok_local, peers, heads_here, head_dim)
    q = queries.reshape(split)
    k = key_vectors.reshape(split)
    v = value_vectors.reshape(split)
    counts = lax.dynamic_slice(block_counts, (me * heads_here,), (heads_here,))

    results = []
    for j in range(heads_here):
        packed = jnp.stack(
            [
                q[:, :, j].transpose(1, 0, 2),
                k[:, :, j].transpose(1, 0, 2),
                v[:, :, j].transpose(1, 2, 0),
            ],
            axis=1,
        )
        tiles = lax.all_to_all(packed, "seq", split_axis=0, concat_axis=0, tiled=True)
        attended = attend(tiles, keep_list[j], counts[j : j + 1], f"head_{j}")
        results.append(lax.all_to_all(attended, "seq", split_axis=0, concat_axis=0, tiled=True))
    together = jnp.stack(results, axis=0)
    return together.transpose(2, 1, 0, 3).reshape(tok_local, head_total * head_dim)


def solution(mesh):
    tokens = P(("batch", "seq"), None)
    return jax.shard_map(
        on_device,
        mesh=mesh,
        in_specs=(tokens, tokens, tokens, tokens, P("batch")),
        out_specs=tokens,
        check_vma=False,
    )
```

time: 326 us -> 160 us (0.49)
  the two profiles are of different devices: /device:TPU:55 before, /device:TPU:1 now
where the time goes in v1:
time: 160 us; the launch traced here: 158 us
  waiting for transfers between devices  73.5 us (46%)
  blocking collectives  31.4 us (20%)
  starting transfers between devices  20.4 us (13%)
  Pallas kernels  16.1 us (10%)
  local copies, waits for them, and re-layouts  12.4 us (8%)
  other arithmetic  3.78 us (2%)
    all_to_all x2, waiting for transfers between devices, on_device(): lax.all_to_all(packed, 'seq', split_axis=0, concat_axis=0, tiled=True)  63.8 us
    all_to_all x1, blocking collectives, on_device(): lax.all_to_all(attended, 'seq', split_axis=0, concat_axis=0, tiled=True)  31.4 us
    pallas_call x2, Pallas kernels, attend(): pl.pallas_call(functools.partial(head_kernel, factor), out_shape=jax.Shap...  16.1 us
    all_to_all x2, starting transfers between devices, on_device(): lax.all_to_all(packed, 'seq', split_axis=0, concat_axis=0, tiled=True)  16.1 us
    all_to_all x1, waiting for transfers between devices, on_device(): lax.all_to_all(attended, 'seq', split_axis=0, concat_axis=0, tiled=True)  9.69 us
    unnamed x13, local copies, waits for them, and re-layouts  7.8 us
    all_to_all x1, starting transfers between devices, on_device(): lax.all_to_all(attended, 'seq', split_axis=0, concat_axis=0, tiled=True)  4.26 us
    another operation x2, other arithmetic, on_device(): jnp.stack([q[:, :, j].transpose(1, 0, 2), k[:, :, j].transpose(1, 0, 2),...  3.68 us
  transfers between devices with their start and end apart: 3, of which 3 were waited for; matrix products, arithmetic and copies ran while one was open for 2% of the time, Pallas kernels for 10%

profile of v1, /device:TPU:1, one launch (start us, length us, event | category | flops | bytes accessed | tf_op | source)
XLA Modules:
  0.0 157.8 jit_solution(74042803748625367)
XLA Ops:
  0.0 1.6 %copy.9 = bf16[128,4096]{0,1:T(8,128)(2,1)S(1)} copy(bf16[128,4096]{1,0:T(8,128)(2,1)} %param.5) | data formatting | bytes 2097152 | tf_op args[0]
  1.6 0.1 fusion
  1.7 0.3 copy.20
  2.0 1.6 %copy.11 = bf16[128,4096]{0,1:T(8,128)(2,1)S(1)} copy(bf16[128,4096]{1,0:T(8,128)(2,1)} %param.6) | data formatting | bytes 2097152 | tf_op args[1]
  3.6 0.9 fusion.1
  4.5 1.3 copy.21
  5.9 1.6 %copy.13 = bf16[128,4096]{0,1:T(8,128)(2,1)S(1)} copy(bf16[128,4096]{1,0:T(8,128)(2,1)} %param.7) | data formatting | bytes 2097152 | tf_op args[2]
  7.5 0.9 slice_bitcast_fusion.1
  8.4 1.3 pad_maximum_fusion
  9.7 11.8 %all-to-all-start = ((bf16[16,3,128,128]{3,2,1,0:T(8,128)(2,1)}), bf16[16,3,128,128]{3,2,1,0:T(8,128)(2,1)S(1)}, u32[]{:S(2)}, u32[]{:S(2)}) async-start(bf16[16,3,128,128]{3,2,1,0:T(8,128)(2,1)} %pad_maximum_fusion), calls=%async_computation | async-start | bytes 3145728 | tf_op jit(solution)/shard_map/all_to_all | solution.py:122
  21.5 0.3 copy.23
  21.8 0.3 copy.24
  22.1 2.4 %pad_maximum_fusion.1 = bf16[16,3,128,128]{3,2,1,0:T(8,128)(2,1)} fusion(bf16[16,1,128,128]{3,2,1,0:T(8,128)(2,1)} %get-tuple-element.10, bf16[16,1,128,128]{3,2,1,0:T(8,128)(2,1)S(1)} %bitcast.56, bf16[16,1,128,128]{3,2,1,0:T(8,128)(2,1)S(1)} %bitcast.55), kind=kLoop, calls=%fused_computation.1 | loop fusion | flops 1572864 | bytes 3145728 | tf_op jit(solution)/shard_map/stack | solution.py:114
  24.4 0.0 copy-start.2
  24.5 0.0 copy-start.1
  24.5 35.5 %all-to-all-done.tiles = bf16[16,3,128,128]{3,2,1,0:T(8,128)(2,1)S(1)} async-done(((bf16[16,3,128,128]{3,2,1,0:T(8,128)(2,1)}), bf16[16,3,128,128]{3,2,1,0:T(8,128)(2,1)S(1)}, u32[]{:S(2)}, u32[]{:S(2)}) %all-to-all-start) | async-done | bytes 1572896 | tf_op jit(solution)/shard_map/all_to_all | solution.py:122
  59.9 4.3 %all-to-all-start.2 = ((bf16[16,3,128,128]{3,2,1,0:T(8,128)(2,1)}), bf16[16,3,128,128]{3,2,1,0:T(8,128)(2,1)S(1)}, u32[]{:S(2)}, u32[]{:S(2)}) async-start(bf16[16,3,128,128]{3,2,1,0:T(8,128)(2,1)} %pad_maximum_fusion.1), calls=%async_computation.2 | async-start | bytes 3145728 | tf_op jit(solution)/shard_map/all_to_all | solution.py:122
  64.2 0.0 copy-done.2
  64.2 0.1 dynamic_slice.3
  64.3 0.7 fusion.2
  65.0 0.0 copy-done.1
  65.0 8.5 %head_0.1 = bf16[16,128,128]{2,1,0:T(8,128)(2,1)S(1)} custom-call(s32[96]{0:T(128)S(1)} %get-tuple-element.11.cells, s32[1]{0:T(128)} %get-tuple-element.13.count, bf16[16,3,128,128]{3,2,1,0:T(8,128)(2,1)S(1)} %all-to-all-done.tiles), custom_call_target="tpu_custom_call" | custom-call | flops 536870912 | bytes 2097152 | tf_op jit(solution)/shard_map/head_0/pallas_call | solution.py:79
  73.5 0.0 copy-start
  73.5 0.8 copy-done
  74.3 28.4 %all-to-all-done.2.tiles = bf16[16,3,128,128]{3,2,1,0:T(8,128)(2,1)S(1)} async-done(((bf16[16,3,128,128]{3,2,1,0:T(8,128)(2,1)}), bf16[16,3,128,128]{3,2,1,0:T(8,128)(2,1)S(1)}, u32[]{:S(2)}, u32[]{:S(2)}) %all-to-all-start.2) | async-done | bytes 1572896 | tf_op jit(solution)/shard_map/all_to_all | solution.py:122
  102.6 4.3 %all-to-all-start.1 = ((bf16[16,128,128]{2,1,0:T(8,128)(2,1)}), bf16[16,128,128]{2,1,0:T(8,128)(2,1)S(1)}, u32[]{:S(2)}, u32[]{:S(2)}) async-start(bf16[16,128,128]{2,1,0:T(8,128)(2,1)} %copy-done), calls=%async_computation.1 | async-start | bytes 1048576 | tf_op jit(solution)/shard_map/all_to_all | solution.py:124
  106.9 7.6 %head_1.1 = bf16[16,128,128]{2,1,0:T(8,128)(2,1)S(1)} custom-call(s32[96]{0:T(128)S(1)} %get-tuple-element.12.cells, s32[1]{0:T(128)} %get-tuple-element.14.count, bf16[16,3,128,128]{3,2,1,0:T(8,128)(2,1)S(1)} %all-to-all-done.2.tiles), custom_call_target="tpu_custom_call" | custom-call | flops 536870912 | bytes 2097152 | tf_op jit(solution)/shard_map/head_1/pallas_call | solution.py:79
  114.5 9.7 %all-to-all-done.1 = bf16[16,128,128]{2,1,0:T(8,128)(2,1)S(1)} async-done(((bf16[16,128,128]{2,1,0:T(8,128)(2,1)}), bf16[16,128,128]{2,1,0:T(8,128)(2,1)S(1)}, u32[]{:S(2)}, u32[]{:S(2)}) %all-to-all-start.1) | async-done | bytes 524320 | tf_op jit(solution)/shard_map/all_to_all | solution.py:124
  124.2 31.4 %all_to_all.20 = bf16[16,128,128]{2,1,0:T(8,128)(2,1)S(1)} all-to-all(bf16[16,128,128]{2,1,0:T(8,128)(2,1)S(1)} %head_1.1), channel_id=1, replica_groups=mesh['seq'=16,'batch'=32] {'seq'}, dimensions={0} | all-to-all | bytes 1048576 | tf_op jit(solution)/shard_map/all_to_all | solution.py:124
  155.7 0.1 maximum_bitcast_fusion
  155.8 0.7 copy.18
  156.4 1.3 copy.19
  (1 shorter events, 0.0 us)
Async XLA Ops:
  9.7 50.3 %all-to-all-start = ((bf16[16,3,128,128]{3,2,1,0:T(8,128)(2,1)}), bf16[16,3,128,128]{3,2,1,0:T(8,128)(2,1)S(1)}, u32[]{:S(2)}, u32[]{:S(2)}) async-start(bf16[16,3,128,128]{3,2,1,0:T(8,128)(2,1)} %pad_maximum_fusion), calls=%async_computation | async-start | bytes 3145728 | tf_op jit(solution)/shard_map/all_to_all | solution.py:122
  24.4 39.8 %copy-start.2 = (s32[32]{0:T(128)S(1)}, s32[32]{0:T(128)}, u32[]{:S(2)}) copy-start(s32[32]{0:T(128)} %param.9) | copy-start | bytes 388
  24.5 40.5 %copy-start.1 = (s32[2,96]{1,0:T(2,128)S(1)}, s32[2,96]{1,0:T(2,128)}, u32[]{:S(2)}) copy-start(s32[2,96]{1,0:T(2,128)} %param.8) | copy-start | bytes 2308
  59.9 42.7 %all-to-all-start.2 = ((bf16[16,3,128,128]{3,2,1,0:T(8,128)(2,1)}), bf16[16,3,128,128]{3,2,1,0:T(8,128)(2,1)S(1)}, u32[]{:S(2)}, u32[]{:S(2)}) async-start(bf16[16,3,128,128]{3,2,1,0:T(8,128)(2,1)} %pad_maximum_fusion.1), calls=%async_computation.2 | async-start | bytes 3145728 | tf_op jit(solution)/shard_map/all_to_all | solution.py:122
  73.5 0.8 copy-start
  102.6 21.6 %all-to-all-start.1 = ((bf16[16,128,128]{2,1,0:T(8,128)(2,1)}), bf16[16,128,128]{2,1,0:T(8,128)(2,1)S(1)}, u32[]{:S(2)}, u32[]{:S(2)}) async-start(bf16[16,128,128]{2,1,0:T(8,128)(2,1)} %copy-done), calls=%async_computation.1 | async-start | bytes 1048576 | tf_op jit(solution)/shard_map/all_to_all | solution.py:124

commit v2 on v1

v2 whole, which is shorter than its diff:
```python
import functools
import math

import jax
import jax.numpy as jnp
from jax import lax
from jax.experimental import pallas as pl
from jax.experimental.pallas import tpu as pltpu
from jax.sharding import PartitionSpec as P

GROUP = 8
neg_large = -1e30
NT = (((1,), (1,)), ((), ()))
NN = (((1,), (0,)), ((), ()))
VMEM = pl.BlockSpec(memory_space=pltpu.VMEM)
SMEM = pl.BlockSpec(memory_space=pltpu.SMEM)
ANY = pl.BlockSpec(memory_space=pl.ANY)


def pack_kernel(first, stride, queries, keys, values, packed, sem):
    peers, _, _, head_dim = packed.shape
    for peer in range(peers):
        column = (peer * stride + first) * head_dim
        for which, source in enumerate((queries, keys, values)):
            pltpu.make_async_copy(
                source.at[:, pl.ds(column, head_dim)], packed.at[peer, which], sem
            ).start()
    pltpu.make_async_copy(packed, packed, sem).wait()


def pack(queries, keys, values, first, stride, peers, head_dim):
    rows = queries.shape[0]
    return pl.pallas_call(
        functools.partial(pack_kernel, first, stride),
        out_shape=jax.ShapeDtypeStruct((peers, 3, rows, head_dim), queries.dtype),
        in_specs=[ANY, ANY, ANY],
        out_specs=ANY,
        scratch_shapes=[pltpu.SemaphoreType.DMA],
        cost_estimate=pl.CostEstimate(
            flops=0, bytes_accessed=6 * peers * 2 * rows * head_dim, transcendentals=0
        ),
        name=f"pack_{first}",
    )(queries, keys, values)


def unpack_kernel(*refs):
    heads, out = refs[:-1], refs[-1]
    peers, _, head_dim = heads[0].shape
    for peer in range(peers):
        for j, head in enumerate(heads):
            column = (peer * len(heads) + j) * head_dim
            out[:, column : column + head_dim] = head[peer]


def unpack(heads):
    peers, rows, head_dim = heads[0].shape
    columns = len(heads) * peers * head_dim
    steps = 4
    return pl.pallas_call(
        unpack_kernel,
        grid=(steps,),
        out_shape=jax.ShapeDtypeStruct((rows, columns), heads[0].dtype),
        in_specs=[pl.BlockSpec((peers // steps, rows, head_dim), lambda i: (i, 0, 0))] * len(heads),
        out_specs=pl.BlockSpec((rows, columns // steps), lambda i: (0, i)),
        name="unpack",
    )(*heads)


def head_kernel(factor, cells, count, tiles, out, values_t, held, held_max, acc, row_max, row_total):
    nblocks = tiles.shape[0]
    live = count[0]

    def score(slot, a, b):
        scores = factor * lax.dot_general(
            tiles[b, 1], tiles[a, 0], NT, preferred_element_type=jnp.float32
        )
        block_max = jnp.max(scores, axis=0, keepdims=True)
        held[slot] = scores
        held_max[slot] = block_max
        return block_max

    def weigh(slot, a, b, is_live):
        block_max = held_max[slot]
        weights = jnp.exp2(held[slot] - block_max)
        share = jnp.exp2(block_max - row_max[a])
        if is_live is not None:
            share = jnp.where(is_live, share, 0.0)
        block_total = jnp.sum(weights, axis=0, keepdims=True)
        block_out = lax.dot_general(
            values_t[b], weights.astype(jnp.bfloat16), NN, preferred_element_type=jnp.float32
        )
        return share * block_total, share * block_out

    def locate(entry):
        cell = cells[jnp.minimum(entry, live - 1)]
        return lax.shift_right_logical(cell, 4), lax.bitwise_and(cell, 15)

    for a in range(nblocks):
        row_max[a] = score(a, a, a)
        values_t[a] = tiles[a, 2].T

    def first_pass(index, carry):
        found = []
        for entry in [index * GROUP + lane for lane in range(GROUP)]:
            a, b = locate(entry)
            found.append((a, score(nblocks + entry, a, b)))
        for a, block_max in found:
            row_max[a] = jnp.maximum(row_max[a], block_max)
        return carry

    steps = (live + GROUP - 1) // GROUP
    lax.fori_loop(0, steps, first_pass, 0)

    for a in range(nblocks):
        row_total[a], acc[a] = weigh(a, a, a, None)

    def second_pass(index, carry):
        found = []
        for entry in [index * GROUP + lane for lane in range(GROUP)]:
            a, b = locate(entry)
            found.append((a, *weigh(nblocks + entry, a, b, entry < live)))
        for a, total, product in found:
            row_total[a] += total
            acc[a] += product
        return carry

    lax.fori_loop(0, steps, second_pass, 0)

    for a in range(nblocks):
        out[a] = (acc[a] / row_total[a]).T.astype(out.dtype)


def attend(tiles, cells, count, name):
    nblocks, _, rows, head_dim = tiles.shape
    factor = head_dim ** (-0.5) * math.log2(math.e)
    slots = nblocks + -(-cells.shape[0] // GROUP) * GROUP
    return pl.pallas_call(
        functools.partial(head_kernel, factor),
        out_shape=jax.ShapeDtypeStruct((nblocks, rows, head_dim), jnp.bfloat16),
        in_specs=[SMEM, SMEM, VMEM],
        out_specs=VMEM,
        scratch_shapes=[
            pltpu.VMEM((nblocks, head_dim, rows), jnp.bfloat16),
            pltpu.VMEM((slots, rows, rows), jnp.float32),
            pltpu.VMEM((slots, 1, rows), jnp.float32),
            pltpu.VMEM((nblocks, head_dim, rows), jnp.float32),
            pltpu.VMEM((nblocks, 1, rows), jnp.float32),
            pltpu.VMEM((nblocks, 1, rows), jnp.float32),
        ],
        compiler_params=pltpu.CompilerParams(vmem_limit_bytes=24 * 1024 * 1024),
        cost_estimate=pl.CostEstimate(
            flops=4 * 64 * rows * rows * head_dim,
            bytes_accessed=2 * 4 * nblocks * rows * head_dim,
            transcendentals=64 * rows * rows,
        ),
        name=name,
    )(cells, count, tiles)


def on_device(queries, key_vectors, value_vectors, keep_list, block_counts):
    peers = lax.axis_size("seq")
    me = lax.axis_index("seq")
    head_total = block_counts.shape[0]
    heads_here = head_total // peers
    head_dim = queries.shape[1] // head_total
    counts = lax.dynamic_slice(block_counts, (me * heads_here,), (heads_here,))

    results = []
    for j in range(heads_here):
        packed = pack(queries, key_vectors, value_vectors, j, heads_here, peers, head_dim)
        tiles = lax.all_to_all(packed, "seq", split_axis=0, concat_axis=0, tiled=True)
        attended = attend(tiles, keep_list[j], counts[j : j + 1], f"head_{j}")
        results.append(lax.all_to_all(attended, "seq", split_axis=0, concat_axis=0, tiled=True))
    return unpack(results)


def solution(mesh):
    tokens = P(("batch", "seq"), None)
    return jax.shard_map(
        on_device,
        mesh=mesh,
        in_specs=(tokens, tokens, tokens, tokens, P("batch")),
        out_specs=tokens,
        check_vma=False,
    )
```

time: 160 us -> 201 us (1.26)
  Pallas kernels: 16.1 us -> 107 us
  waiting for transfers between devices: 73.5 us -> 48.2 us
  blocking collectives: 31.4 us -> 20 us
  local copies, waits for them, and re-layouts: 12.4 us -> 1.47 us
  other arithmetic: 3.78 us -> 0 us
  starting transfers between devices: 20.4 us -> 23.3 us
    pallas_call x0 -> x3, Pallas kernels: none -> 101 us  [the longest x2 97.5 us: pack(): pl.pallas_call(functools.partial(pack_kernel, first, stride), out_shape=j...]
    all_to_all x2, waiting for transfers between devices: 63.8 us -> 34.2 us  [on_device(): lax.all_to_all(packed, 'seq', split_axis=0, concat_axis=0, tiled=True)]
    all_to_all x1, blocking collectives: 31.4 us -> 20 us  [on_device(): lax.all_to_all(attended, 'seq', split_axis=0, concat_axis=0, tiled=True)]
    pallas_call x2, Pallas kernels: 16.1 us -> 6.09 us  [attend(): pl.pallas_call(functools.partial(head_kernel, factor), out_shape=jax.Shap...]
    unnamed x13 -> x8, local copies, waits for them, and re-layouts: 7.8 us -> 0.8 us
    all_to_all x1, waiting for transfers between devices: 9.69 us -> 14 us  [on_device(): lax.all_to_all(attended, 'seq', split_axis=0, concat_axis=0, tiled=True)]
    another operation x2 -> x0, other arithmetic: 3.68 us -> none  [on_device(): jnp.stack([q[:, :, j].transpose(1, 0, 2), k[:, :, j].transpose(1, 0, 2),...]
    all_to_all x2, starting transfers between devices: 16.1 us -> 19.1 us  [on_device(): lax.all_to_all(packed, 'seq', split_axis=0, concat_axis=0, tiled=True)]
  transfers between devices with their start and end apart: 3 -> 3, of which waited for: 3 -> 2; matrix products, arithmetic and copies ran while one was open for 2% -> 0% of each run, Pallas kernels for 10% -> 27%
where the time goes in v2:
time: 201 us; the launch traced here: 200 us
  Pallas kernels  107 us (53%)
  waiting for transfers between devices  48.2 us (24%)
  starting transfers between devices  23.3 us (12%)
  blocking collectives  20 us (10%)
    pallas_call x2, Pallas kernels, pack(): pl.pallas_call(functools.partial(pack_kernel, first, stride), out_shape=j...  97.5 us
    all_to_all x2, waiting for transfers between devices, on_device(): lax.all_to_all(packed, 'seq', split_axis=0, concat_axis=0, tiled=True)  34.2 us
    all_to_all x1, blocking collectives, on_device(): lax.all_to_all(attended, 'seq', split_axis=0, concat_axis=0, tiled=True)  20 us
    all_to_all x2, starting transfers between devices, on_device(): lax.all_to_all(packed, 'seq', split_axis=0, concat_axis=0, tiled=True)  19.1 us
    all_to_all x1, waiting for transfers between devices, on_device(): lax.all_to_all(attended, 'seq', split_axis=0, concat_axis=0, tiled=True)  14 us
    pallas_call x2, Pallas kernels, attend(): pl.pallas_call(functools.partial(head_kernel, factor), out_shape=jax.Shap...  6.09 us
    all_to_all x1, starting transfers between devices, on_device(): lax.all_to_all(attended, 'seq', split_axis=0, concat_axis=0, tiled=True)  4.26 us
  transfers between devices with their start and end apart: 3, of which 2 were waited for; matrix products, arithmetic and copies ran while one was open for 0% of the time, Pallas kernels for 27%

profile of v2, /device:TPU:1, one launch (start us, length us, event | category | flops | bytes accessed | tf_op | source)
XLA Modules:
  0.0 200.2 jit_solution(12045925545736243784)
XLA Ops:
  0.0 48.8 %pack_1.1 = bf16[16,3,128,128]{3,2,1,0:T(8,128)(2,1)} custom-call(bf16[128,4096]{1,0:T(8,128)(2,1)} %queries.3, bf16[128,4096]{1,0:T(8,128)(2,1)} %keys.3, bf16[128,4096]{1,0:T(8,128)(2,1)} %values.3), custom_call_target="tpu_custom_call" | custom-call | bytes 3145728 | tf_op jit(solution)/shard_map/pack_1/pallas_call | solution.py:33
  48.8 11.8 %all-to-all-start.2 = ((bf16[16,3,128,128]{3,2,1,0:T(8,128)(2,1)}), bf16[16,3,128,128]{3,2,1,0:T(8,128)(2,1)S(1)}, u32[]{:S(2)}, u32[]{:S(2)}) async-start(bf16[16,3,128,128]{3,2,1,0:T(8,128)(2,1)} %pack_1.1), calls=%async_computation.2 | async-start | bytes 3145728 | tf_op jit(solution)/shard_map/all_to_all | solution.py:171
  60.6 48.8 %pack_0.1 = bf16[16,3,128,128]{3,2,1,0:T(8,128)(2,1)} custom-call(bf16[128,4096]{1,0:T(8,128)(2,1)} %queries.3, bf16[128,4096]{1,0:T(8,128)(2,1)} %keys.3, bf16[128,4096]{1,0:T(8,128)(2,1)} %values.3), custom_call_target="tpu_custom_call" | custom-call | bytes 3145728 | tf_op jit(solution)/shard_map/pack_0/pallas_call | solution.py:33
  109.4 0.0 copy-start.3
  109.4 0.0 copy-start.2
  109.4 0.0 all-to-all-done.2.tiles
  109.4 7.2 %all-to-all-start = ((bf16[16,3,128,128]{3,2,1,0:T(8,128)(2,1)}), bf16[16,3,128,128]{3,2,1,0:T(8,128)(2,1)S(1)}, u32[]{:S(2)}, u32[]{:S(2)}) async-start(bf16[16,3,128,128]{3,2,1,0:T(8,128)(2,1)} %pack_0.1), calls=%async_computation | async-start | bytes 3145728 | tf_op jit(solution)/shard_map/all_to_all | solution.py:171
  116.6 0.0 copy-done.3
  116.6 0.1 dynamic_slice.3
  116.7 0.6 fusion
  117.3 0.0 copy-done.2
  117.3 2.8 %head_1.1 = bf16[16,128,128]{2,1,0:T(8,128)(2,1)S(1)} custom-call(s32[96]{0:T(128)S(1)} %get-tuple-element.5.cells, s32[1]{0:T(128)} %get-tuple-element.7.count, bf16[16,3,128,128]{3,2,1,0:T(8,128)(2,1)S(1)} %all-to-all-done.2.tiles), custom_call_target="tpu_custom_call" | custom-call | flops 536870912 | bytes 2097152 | tf_op jit(solution)/shard_map/head_1/pallas_call | solution.py:137
  120.1 0.0 copy-start
  120.1 0.8 copy-done
  120.9 34.2 %all-to-all-done.tiles = bf16[16,3,128,128]{3,2,1,0:T(8,128)(2,1)S(1)} async-done(((bf16[16,3,128,128]{3,2,1,0:T(8,128)(2,1)}), bf16[16,3,128,128]{3,2,1,0:T(8,128)(2,1)S(1)}, u32[]{:S(2)}, u32[]{:S(2)}) %all-to-all-start) | async-done | bytes 1572896 | tf_op jit(solution)/shard_map/all_to_all | solution.py:171
  155.1 4.3 %all-to-all-start.3 = ((bf16[16,128,128]{2,1,0:T(8,128)(2,1)}), bf16[16,128,128]{2,1,0:T(8,128)(2,1)S(1)}, u32[]{:S(2)}, u32[]{:S(2)}) async-start(bf16[16,128,128]{2,1,0:T(8,128)(2,1)} %copy-done), calls=%async_computation.3 | async-start | bytes 1048576 | tf_op jit(solution)/shard_map/all_to_all | solution.py:173
  159.3 3.3 %head_0.1 = bf16[16,128,128]{2,1,0:T(8,128)(2,1)S(1)} custom-call(s32[96]{0:T(128)S(1)} %get-tuple-element.6.cells, s32[1]{0:T(128)} %get-tuple-element.8.count, bf16[16,3,128,128]{3,2,1,0:T(8,128)(2,1)S(1)} %all-to-all-done.tiles), custom_call_target="tpu_custom_call" | custom-call | flops 536870912 | bytes 2097152 | tf_op jit(solution)/shard_map/head_0/pallas_call | solution.py:137
  162.7 14.0 %all-to-all-done.3.refs_1_ = bf16[16,128,128]{2,1,0:T(8,128)(2,1)S(1)} async-done(((bf16[16,128,128]{2,1,0:T(8,128)(2,1)}), bf16[16,128,128]{2,1,0:T(8,128)(2,1)S(1)}, u32[]{:S(2)}, u32[]{:S(2)}) %all-to-all-start.3) | async-done | bytes 524320 | tf_op jit(solution)/shard_map/all_to_all | solution.py:173
  176.7 0.0 copy-start.1
  176.7 20.0 %all_to_all.20.refs_0_ = bf16[16,128,128]{2,1,0:T(8,128)(2,1)} all-to-all(bf16[16,128,128]{2,1,0:T(8,128)(2,1)S(1)} %head_0.1), channel_id=1, replica_groups=mesh['seq'=16,'batch'=32] {'seq'}, dimensions={0} | all-to-all | bytes 1048576 | tf_op jit(solution)/shard_map/all_to_all | solution.py:173
  196.7 0.0 copy-done.1
  196.7 3.5 %unpack.1 = bf16[128,4096]{1,0:T(8,128)(2,1)} custom-call(bf16[16,128,128]{2,1,0:T(8,128)(2,1)} %all_to_all.20.refs_0_, bf16[16,128,128]{2,1,0:T(8,128)(2,1)} %copy-done.1), custom_call_target="tpu_custom_call" | custom-call | tf_op jit(solution)/shard_map/unpack/pallas_call | solution.py:59
  (1 shorter events, 0.0 us)
Async XLA Ops:
  48.8 60.6 %all-to-all-start.2 = ((bf16[16,3,128,128]{3,2,1,0:T(8,128)(2,1)}), bf16[16,3,128,128]{3,2,1,0:T(8,128)(2,1)S(1)}, u32[]{:S(2)}, u32[]{:S(2)}) async-start(bf16[16,3,128,128]{3,2,1,0:T(8,128)(2,1)} %pack_1.1), calls=%async_computation.2 | async-start | bytes 3145728 | tf_op jit(solution)/shard_map/all_to_all | solution.py:171
  109.4 7.3 %copy-start.3 = (s32[32]{0:T(128)S(1)}, s32[32]{0:T(128)}, u32[]{:S(2)}) copy-start(s32[32]{0:T(128)} %param.9) | copy-start | bytes 388
  109.4 7.9 %copy-start.2 = (s32[2,96]{1,0:T(2,128)S(1)}, s32[2,96]{1,0:T(2,128)}, u32[]{:S(2)}) copy-start(s32[2,96]{1,0:T(2,128)} %param.8) | copy-start | bytes 2308
  109.4 45.7 %all-to-all-start = ((bf16[16,3,128,128]{3,2,1,0:T(8,128)(2,1)}), bf16[16,3,128,128]{3,2,1,0:T(8,128)(2,1)S(1)}, u32[]{:S(2)}, u32[]{:S(2)}) async-start(bf16[16,3,128,128]{3,2,1,0:T(8,128)(2,1)} %pack_0.1), calls=%async_computation | async-start | bytes 3145728 | tf_op jit(solution)/shard_map/all_to_all | solution.py:171
  120.1 0.8 copy-start
  155.1 21.6 %all-to-all-start.3 = ((bf16[16,128,128]{2,1,0:T(8,128)(2,1)}), bf16[16,128,128]{2,1,0:T(8,128)(2,1)S(1)}, u32[]{:S(2)}, u32[]{:S(2)}) async-start(bf16[16,128,128]{2,1,0:T(8,128)(2,1)} %copy-done), calls=%async_computation.3 | async-start | bytes 1048576 | tf_op jit(solution)/shard_map/all_to_all | solution.py:173
  176.7 20.0 %copy-start.1 = (bf16[16,128,128]{2,1,0:T(8,128)(2,1)}, bf16[16,128,128]{2,1,0:T(8,128)(2,1)S(1)}, u32[]{:S(2)}) copy-start(bf16[16,128,128]{2,1,0:T(8,128)(2,1)S(1)} %all-to-all-done.3.refs_1_) | copy-start | bytes 1572868

commit v3 on v2

v3 whole, which is shorter than its diff:
```python
import functools
import math

import jax
import jax.numpy as jnp
from jax import lax
from jax.experimental import pallas as pl
from jax.experimental.pallas import tpu as pltpu
from jax.sharding import PartitionSpec as P

GROUP = 8
CHUNKS = 8
KINDS = 3
LIST_ROWS = 16
NT = (((1,), (1,)), ((), ()))
NN = (((1,), (0,)), ((), ()))
VMEM = pl.BlockSpec(memory_space=pltpu.VMEM)
SMEM = pl.BlockSpec(memory_space=pltpu.SMEM)
ANY = pl.BlockSpec(memory_space=pl.ANY)


def rank_to_place(rank, peers):
    j = rank // peers
    peer = rank - j * peers
    return jnp.where(j % 2 == 0, peer, peers - 1 - peer), j


def place_to_rank(peer, j, peers):
    return j * peers + (peer if j % 2 == 0 else peers - 1 - peer)


def tile_rows(j, kind, rows):
    return pl.ds(pl.multiple_of((j * KINDS + kind) * rows, rows), rows)


def pack_kernel(
    counts, lists, queries, keys, values, packed, order, came, goes, gone_lists, list_tile_ref, keys_of, ranks, came_sems, goes_sem
):
    peers, _, head_dim = packed.shape
    head_total = counts.shape[0]
    rows = queries.shape[0]
    per_chunk = head_total // CHUNKS
    sources = (queries, keys, values)
    copies = []
    for chunk in range(CHUNKS):
        span = pl.ds(chunk * per_chunk * head_dim, per_chunk * head_dim)
        for kind, source in enumerate(sources):
            copy = pltpu.make_async_copy(
                source.at[:, span], came.at[kind, :, span], came_sems.at[chunk, kind]
            )
            copy.start()
            copies.append(copy)

    gone_lists[...] = jnp.zeros_like(gone_lists)
    gone_lists[: lists.shape[0], : lists.shape[1]] = lists[...].astype(jnp.float32)
    list_tile_ref[...] = gone_lists[...].astype(packed.dtype)
    for peer in range(peers):
        pltpu.make_async_copy(
            list_tile_ref, packed.at[peer, pl.ds(head_total // peers * KINDS * rows, LIST_ROWS)], goes_sem
        ).start()

    for head in range(head_total):
        keys_of[head] = counts[head] * head_total - head

    def find_rank(head, carry):
        mine = keys_of[head]
        rank = jnp.int32(0)
        for other in range(head_total):
            rank += (keys_of[other] > mine).astype(jnp.int32)
        ranks[head] = rank
        order[rank] = head
        return carry

    lax.fori_loop(0, head_total, find_rank, 0)

    for head in range(head_total):
        chunk, first = divmod(head, per_chunk)
        for kind in range(len(sources)):
            if first == 0:
                copies[chunk * len(sources) + kind].wait()
            goes[head, kind * rows : (kind + 1) * rows] = came[
                kind, :, head * head_dim : (head + 1) * head_dim
            ]
        peer, j = rank_to_place(ranks[head], peers)
        span = pl.ds(pl.multiple_of(j * KINDS * rows, rows), KINDS * rows)
        pltpu.make_async_copy(goes.at[head], packed.at[peer, span], goes_sem).start()
    pltpu.make_async_copy(packed, packed, goes_sem).wait()


def pack(counts, lists, queries, keys, values, peers):
    rows, columns = queries.shape
    head_total = counts.shape[0]
    head_dim = columns // head_total
    heads_here = head_total // peers
    parcel_rows = heads_here * KINDS * rows + LIST_ROWS
    return pl.pallas_call(
        pack_kernel,
        out_shape=(
            jax.ShapeDtypeStruct((peers, parcel_rows, head_dim), queries.dtype),
            jax.ShapeDtypeStruct((head_total,), jnp.int32),
        ),
        in_specs=[SMEM, VMEM, ANY, ANY, ANY],
        out_specs=(ANY, SMEM),
        scratch_shapes=[
            pltpu.VMEM((KINDS, rows, columns), queries.dtype),
            pltpu.VMEM((head_total, KINDS * rows, head_dim), queries.dtype),
            pltpu.VMEM((LIST_ROWS, head_dim), jnp.float32),
            pltpu.VMEM((LIST_ROWS, head_dim), queries.dtype),
            pltpu.SMEM((head_total,), jnp.int32),
            pltpu.SMEM((head_total,), jnp.int32),
            pltpu.SemaphoreType.DMA((CHUNKS, KINDS)),
            pltpu.SemaphoreType.DMA,
        ],
        compiler_params=pltpu.CompilerParams(vmem_limit_bytes=60 * 1024 * 1024),
        name="pack",
    )(counts, lists, queries, keys, values)


def unpack_kernel(order, heads, out, staged, sems):
    peers, heads_here, rows, head_dim = heads.shape
    step = rows // CHUNKS
    copies = []
    for chunk in range(CHUNKS):
        span = pl.ds(chunk * step, step)
        for peer in range(peers):
            for j in range(heads_here):
                head = order[place_to_rank(peer, j, peers)]
                column = pl.multiple_of(head * head_dim, head_dim)
                staged[span, pl.ds(column, head_dim)] = heads[peer, j, span, :]
        copy = pltpu.make_async_copy(staged.at[span, :], out.at[span, :], sems.at[chunk])
        copy.start()
        copies.append(copy)
    for copy in copies:
        copy.wait()


def unpack(order, heads):
    peers, heads_here, rows, head_dim = heads.shape
    columns = peers * heads_here * head_dim
    return pl.pallas_call(
        unpack_kernel,
        out_shape=jax.ShapeDtypeStruct((rows, columns), heads.dtype),
        in_specs=[SMEM, VMEM],
        out_specs=ANY,
        scratch_shapes=[
            pltpu.VMEM((rows, columns), heads.dtype),
            pltpu.SemaphoreType.DMA((CHUNKS,)),
        ],
        compiler_params=pltpu.CompilerParams(vmem_limit_bytes=8 * 1024 * 1024),
        name="unpack",
    )(order, heads)


def heads_kernel(
    factor,
    me,
    order,
    all_counts,
    parcels,
    out,
    values_t,
    held,
    held_max,
    acc,
    row_max,
    row_total,
    came_lists,
    cells,
    lists_sem,
):
    nblocks, heads_here, rows, _ = out.shape
    grid_rows = nblocks * heads_here
    peers = order.shape[0] // heads_here
    lists_at = heads_here * KINDS * rows
    for sender in range(peers):
        numbers = parcels[sender, pl.ds(lists_at, LIST_ROWS), :].astype(jnp.float32)
        came_lists[pl.ds(sender * 8, 8)] = numbers[:8].astype(jnp.int32)
    lists_copy = pltpu.make_async_copy(came_lists, cells, lists_sem)
    lists_copy.start()
    heads = [order[place_to_rank(me[0], j, peers)] for j in range(heads_here)]
    counts = [all_counts[head] for head in heads]
    live = functools.reduce(lambda x, y: x + y, counts)

    def score(slot, j, a, b):
        scores = factor * lax.dot_general(
            parcels[b, tile_rows(j, 1, rows), :],
            parcels[a, tile_rows(j, 0, rows), :],
            NT,
            preferred_element_type=jnp.float32,
        )
        block_max = jnp.max(scores, axis=0, keepdims=True)
        held[slot] = scores
        held_max[slot] = block_max
        return block_max

    def weigh(slot, j, a, b, is_live):
        block_max = held_max[slot]
        weights = jnp.exp2(held[slot] - block_max)
        share = jnp.exp2(block_max - row_max[j * nblocks + a])
        if is_live is not None:
            share = jnp.where(is_live, share, 0.0)
        block_total = jnp.sum(weights, axis=0, keepdims=True)
        block_out = lax.dot_general(
            values_t[j * nblocks + b],
            weights.astype(jnp.bfloat16),
            NN,
            preferred_element_type=jnp.float32,
        )
        return share * block_total, share * block_out

    def locate(entry):
        entry = jnp.minimum(entry, live - 1)
        j = jnp.int32(0)
        head = heads[0]
        place = entry
        for later in range(1, heads_here):
            entry -= counts[later - 1]
            j = jnp.where(entry >= 0, later, j)
            head = jnp.where(entry >= 0, heads[later], head)
            place = jnp.where(entry >= 0, entry, place)
        sender = head // heads_here
        cell = cells[sender * 8 + (head - sender * heads_here), place]
        return j, lax.shift_right_logical(cell, 4), lax.bitwise_and(cell, 15)

    for j in range(heads_here):
        for a in range(nblocks):
            row = j * nblocks + a
            row_max[row] = score(row, j, a, a)
            values_t[row] = parcels[a, tile_rows(j, 2, rows), :].T

    def first_pass(index, carry):
        found = []
        for entry in [index * GROUP + lane for lane in range(GROUP)]:
            j, a, b = locate(entry)
            found.append((j * nblocks + a, score(grid_rows + entry, j, a, b)))
        for row, block_max in found:
            row_max[row] = jnp.maximum(row_max[row], block_max)
        return carry

    steps = (live + GROUP - 1) // GROUP
    lists_copy.wait()
    lax.fori_loop(0, steps, first_pass, 0)

    for j in range(heads_here):
        for a in range(nblocks):
            row = j * nblocks + a
            row_total[row], acc[row] = weigh(row, j, a, a, None)

    def second_pass(index, carry):
        found = []
        for entry in [index * GROUP + lane for lane in range(GROUP)]:
            j, a, b = locate(entry)
            found.append((j * nblocks + a, *weigh(grid_rows + entry, j, a, b, entry < live)))
        for row, total, product in found:
            row_total[row] += total
            acc[row] += product
        return carry

    lax.fori_loop(0, steps, second_pass, 0)

    for j in range(heads_here):
        for a in range(nblocks):
            row = j * nblocks + a
            out[a, j] = (acc[row] / row_total[row]).T.astype(out.dtype)


def attend(me, order, counts, parcels, list_len):
    nblocks, parcel_rows, head_dim = parcels.shape
    peers = nblocks
    heads_here = counts.shape[0] // peers
    rows = (parcel_rows - LIST_ROWS) // (heads_here * KINDS)
    factor = head_dim ** (-0.5) * math.log2(math.e)
    grid_rows = nblocks * heads_here
    slots = grid_rows + -(-list_len * heads_here // GROUP) * GROUP
    return pl.pallas_call(
        functools.partial(heads_kernel, factor),
        out_shape=jax.ShapeDtypeStruct((nblocks, heads_here, rows, head_dim), jnp.bfloat16),
        in_specs=[SMEM, SMEM, SMEM, VMEM],
        out_specs=VMEM,
        scratch_shapes=[
            pltpu.VMEM((grid_rows, head_dim, rows), jnp.bfloat16),
            pltpu.VMEM((slots, rows, rows), jnp.float32),
            pltpu.VMEM((slots, 1, rows), jnp.float32),
            pltpu.VMEM((grid_rows, head_dim, rows), jnp.float32),
            pltpu.VMEM((grid_rows, 1, rows), jnp.float32),
            pltpu.VMEM((grid_rows, 1, rows), jnp.float32),
            pltpu.VMEM((peers * 8, head_dim), jnp.int32),
            pltpu.SMEM((peers * 8, head_dim), jnp.int32),
            pltpu.SemaphoreType.DMA,
        ],
        compiler_params=pltpu.CompilerParams(vmem_limit_bytes=36 * 1024 * 1024),
        name="attend",
    )(me, order, counts, parcels)


def on_device(queries, key_vectors, value_vectors, keep_list, block_counts):
    peers = lax.axis_size("seq")
    me = lax.axis_index("seq")
    packed, order = pack(
        block_counts, keep_list, queries, key_vectors, value_vectors, peers
    )
    parcels = lax.all_to_all(packed, "seq", split_axis=0, concat_axis=0, tiled=True)
    attended = attend(me.reshape(1), order, block_counts, parcels, keep_list.shape[1])
    returned = lax.all_to_all(attended, "seq", split_axis=0, concat_axis=0, tiled=True)
    return unpack(order, returned)


def solution(mesh):
    tokens = P(("batch", "seq"), None)
    return jax.shard_map(
        on_device,
        mesh=mesh,
        in_specs=(tokens, tokens, tokens, tokens, P("batch")),
        out_specs=tokens,
        check_vma=False,
    )
```

time: 201 us -> 134 us (0.67)
  Pallas kernels: 107 us -> 17 us
  waiting for transfers between devices: 48.2 us -> 72.4 us
  blocking collectives: 20 us -> 32.5 us
  starting transfers between devices: 23.3 us -> 11.8 us
    pallas_call x5 -> x3, Pallas kernels: 107 us -> 17 us  [the longest x1 10.7 us: attend(): pl.pallas_call(functools.partial(heads_kernel, factor), out_shape=jax.Sha...]
    all_to_all x2 -> x1, waiting for transfers between devices: 34.2 us -> 72.4 us  [on_device(): lax.all_to_all(packed, 'seq', split_axis=0, concat_axis=0, tiled=True)]
    all_to_all x1 -> x0, waiting for transfers between devices: 14 us -> none  [on_device(): lax.all_to_all(attended, 'seq', split_axis=0, concat_axis=0, tiled=True)]
    all_to_all x1, blocking collectives: 20 us -> 32.5 us  [on_device(): lax.all_to_all(attended, 'seq', split_axis=0, concat_axis=0, tiled=True)]
    all_to_all x2 -> x1, starting transfers between devices: 19.1 us -> 11.8 us  [on_device(): lax.all_to_all(packed, 'seq', split_axis=0, concat_axis=0, tiled=True)]
    all_to_all x1 -> x0, starting transfers between devices: 4.26 us -> none  [on_device(): lax.all_to_all(attended, 'seq', split_axis=0, concat_axis=0, tiled=True)]
  transfers between devices with their start and end apart: 3 -> 1, of which waited for: 2 -> 1; matrix products, arithmetic and copies ran while one was open for 0% -> 0% of each run, Pallas kernels for 27% -> 0%
where the time goes in v3:
time: 134 us
  waiting for transfers between devices  72.4 us (54%)
  blocking collectives  32.5 us (24%)
  Pallas kernels  17 us (13%)
  starting transfers between devices  11.8 us (9%)
    all_to_all x1, waiting for transfers between devices, on_device(): lax.all_to_all(packed, 'seq', split_axis=0, concat_axis=0, tiled=True)  72.4 us
    all_to_all x1, blocking collectives, on_device(): lax.all_to_all(attended, 'seq', split_axis=0, concat_axis=0, tiled=True)  32.5 us
    all_to_all x1, starting transfers between devices, on_device(): lax.all_to_all(packed, 'seq', split_axis=0, concat_axis=0, tiled=True)  11.8 us
    pallas_call x1, Pallas kernels, attend(): pl.pallas_call(functools.partial(heads_kernel, factor), out_shape=jax.Sha...  10.7 us
    pallas_call x1, Pallas kernels, pack(): pl.pallas_call(pack_kernel, out_shape=(jax.ShapeDtypeStruct((peers, parce...  4.74 us
  transfers between devices with their start and end apart: 1, of which 1 were waited for; matrix products, arithmetic and copies ran while one was open for 0% of the time, Pallas kernels for 0%

profile of v3, /device:TPU:1, one launch (start us, length us, event | category | flops | bytes accessed | tf_op | source)
XLA Modules:
  0.0 133.8 jit_solution(9075426753086213809)
XLA Ops:
  0.0 4.7 %pack.1 = (bf16[16,784,128]{2,1,0:T(8,128)(2,1)}, s32[32]{0:T(128)}) custom-call(s32[32]{0:T(128)} %all_counts.1, s32[2,96]{1,0:T(2,128)} %lists.1, bf16[128,4096]{1,0:T(8,128)(2,1)} %queries.1, bf16[128,4096]{1,0:T(8,128)(2,1)} %keys.1, bf16[128,4096]{1,0:T(8,128)(2,1)} %values.1), custom_call_target="tpu_custom_call" | custom-call | tf_op jit(solution)/shard_map/pack/pallas_call | solution.py:96
  4.7 0.0 copy-start
  4.8 0.0 copy-start.1
  4.8 11.8 %all-to-all-start = ((bf16[16,784,128]{2,1,0:T(8,128)(2,1)}), bf16[16,784,128]{2,1,0:T(8,128)(2,1)S(1)}, u32[]{:S(2)}, u32[]{:S(2)}) async-start(bf16[16,784,128]{2,1,0:T(8,128)(2,1)} %get-tuple-element.8), calls=%async_computation | async-start | bytes 6422528 | tf_op jit(solution)/shard_map/all_to_all | solution.py:302
  16.6 72.4 %all-to-all-done.parcels = bf16[16,784,128]{2,1,0:T(8,128)(2,1)S(1)} async-done(((bf16[16,784,128]{2,1,0:T(8,128)(2,1)}), bf16[16,784,128]{2,1,0:T(8,128)(2,1)S(1)}, u32[]{:S(2)}, u32[]{:S(2)}) %all-to-all-start) | async-done | bytes 3211296 | tf_op jit(solution)/shard_map/all_to_all | solution.py:302
  89.0 0.0 copy-done
  89.0 0.0 copy-done.1
  89.1 10.7 %attend.1 = bf16[16,2,128,128]{3,2,1,0:T(8,128)(2,1)S(1)} custom-call(s32[1]{0:T(128)} %bitcast.me, s32[32]{0:T(128)S(1)} %copy-done.1, s32[32]{0:T(128)S(1)} %copy-done, bf16[16,784,128]{2,1,0:T(8,128)(2,1)S(1)} %all-to-all-done.parcels), custom_call_target="tpu_custom_call" | custom-call | tf_op jit(solution)/shard_map/attend/pallas_call | solution.py:275
  99.8 32.5 %all_to_all.10.heads = bf16[16,2,128,128]{3,2,1,0:T(8,128)(2,1)S(1)} all-to-all(bf16[16,2,128,128]{3,2,1,0:T(8,128)(2,1)S(1)} %attend.1), channel_id=1, replica_groups=mesh['seq'=16,'batch'=32] {'seq'}, dimensions={0} | all-to-all | bytes 2097152 | tf_op jit(solution)/shard_map/all_to_all | solution.py:304
  132.2 1.6 %unpack.1 = bf16[128,4096]{1,0:T(8,128)(2,1)} custom-call(s32[32]{0:T(128)S(1)} %copy-done.1, bf16[16,2,128,128]{3,2,1,0:T(8,128)(2,1)S(1)} %all_to_all.10.heads), custom_call_target="tpu_custom_call" | custom-call | tf_op jit(solution)/shard_map/unpack/pallas_call | solution.py:140
Async XLA Ops:
  4.7 84.3 %copy-start = (s32[32]{0:T(128)S(1)}, s32[32]{0:T(128)}, u32[]{:S(2)}) copy-start(s32[32]{0:T(128)} %all_counts.1) | copy-start | bytes 388
  4.8 84.3 %copy-start.1 = (s32[32]{0:T(128)S(1)}, s32[32]{0:T(128)}, u32[]{:S(2)}) copy-start(s32[32]{0:T(128)} %get-tuple-element.7.order) | copy-start | bytes 388
  4.8 84.3 %all-to-all-start = ((bf16[16,784,128]{2,1,0:T(8,128)(2,1)}), bf16[16,784,128]{2,1,0:T(8,128)(2,1)S(1)}, u32[]{:S(2)}, u32[]{:S(2)}) async-start(bf16[16,784,128]{2,1,0:T(8,128)(2,1)} %get-tuple-element.8), calls=%async_computation | async-start | bytes 6422528 | tf_op jit(solution)/shard_map/all_to_all | solution.py:302

commit v4 on v3

v4 whole, which is shorter than its diff:
```python
import functools
import math

import jax
import jax.numpy as jnp
from jax import lax
from jax.experimental import pallas as pl
from jax.experimental.pallas import tpu as pltpu
from jax.sharding import PartitionSpec as P

GROUP = 16
NONE = 16
CHUNKS = 8
LOADS = 4
KINDS = 3
PAIR_ROWS = 8
LIST_ROWS = 16
NT = (((1,), (1,)), ((), ()))
NN = (((1,), (0,)), ((), ()))
VMEM = pl.BlockSpec(memory_space=pltpu.VMEM)
SMEM = pl.BlockSpec(memory_space=pltpu.SMEM)
ANY = pl.BlockSpec(memory_space=pl.ANY)


def rank_to_place(rank, peers):
    j = rank // peers
    peer = rank - j * peers
    return jnp.where(j % 2 == 0, peer, peers - 1 - peer), j


def place_to_rank(peer, j, peers):
    return j * peers + (peer if j % 2 == 0 else peers - 1 - peer)


def tile_rows(j, kind, rows):
    return pl.ds(pl.multiple_of((j * KINDS + kind) * rows, rows), rows)


def small_product(left, right):
    return jnp.dot(
        left.astype(jnp.bfloat16), right.astype(jnp.bfloat16), preferred_element_type=jnp.float32
    )


def pair_tables(lists, list_len, live):
    lines, size = lists.shape
    across = lax.broadcasted_iota(jnp.int32, (size, size), 1)
    down = lax.broadcasted_iota(jnp.int32, (size, size), 0)
    lane = lax.broadcasted_iota(jnp.int32, (lines, size), 1)
    line = lax.broadcasted_iota(jnp.int32, (lines, size), 0)
    across_f = across.astype(jnp.float32)
    on_diagonal = (lane >= list_len) & (lane < list_len + 16)
    cell = jnp.where(on_diagonal, (lane - list_len) * 17, lists)
    listed = functools.reduce(lambda x, y: x | y, [(line == j) & (lane < c) for j, c in enumerate(live)])
    row = lax.shift_right_logical(cell, 4).astype(jnp.float32)
    column = jnp.where(on_diagonal | listed, lax.bitwise_and(cell, 15), size).astype(jnp.float32)
    upright = jnp.concatenate([column, row, jnp.zeros((size - 2 * lines, size), jnp.float32)], axis=0).T
    members = [(upright[:, j : j + 1] == across_f).astype(jnp.float32) for j in range(len(live))]
    counted = small_product((across < down).astype(jnp.float32), jnp.concatenate(members, axis=1))
    pairs = [jnp.floor((jnp.sum(member, axis=0, keepdims=True) + 1.0) * 0.5) for member in members]
    pairs_lines = functools.reduce(
        lambda x, y: x + y, [jnp.where(line == j, p, 0.0) for j, p in enumerate(pairs)]
    )
    firsts = small_product(pairs_lines, (down < across).astype(jnp.float32))
    tables = []
    for j, member in enumerate(members):
        earlier = jnp.sum(member * counted[:, j * size : (j + 1) * size], axis=1, keepdims=True)
        half = jnp.floor(earlier * 0.5)
        place = jnp.sum(member * firsts[j : j + 1], axis=1, keepdims=True) + half
        here = jnp.where(place == across_f, jnp.sum(member, axis=1, keepdims=True), 0.0)
        second = earlier - 2.0 * half
        picks = jnp.concatenate([here * (1.0 - second), here * second], axis=1)
        own_column, own_row = column[j : j + 1], row[j : j + 1]
        facts = jnp.where(line == 0, own_column, jnp.where(line == 1, own_row, own_row - NONE))
        found = small_product(facts, picks)
        total = jnp.sum(pairs[j], axis=1, keepdims=True)
        tables.append(
            jnp.where(
                line < 2, found[:, :size], jnp.where(line == 2, found[:, size:] + NONE, total)
            )
        )
    return jnp.concatenate(tables, axis=0)


def pack_kernel(
    me, counts, lists, queries, keys, values, packed, order, came, goes, wide_lists, gone_tables, came_sems, goes_sem
):
    peers, _, head_dim = packed.shape
    head_total = counts.shape[0]
    rows = queries.shape[0]
    per_chunk = head_total // LOADS
    sources = (queries, keys, values)
    copies = []
    for chunk in range(LOADS):
        span = pl.ds(chunk * per_chunk * head_dim, per_chunk * head_dim)
        for kind, source in enumerate(sources):
            copy = pltpu.make_async_copy(
                source.at[:, span], came.at[kind, :, span], came_sems.at[chunk, kind]
            )
            copy.start()
            copies.append(copy)

    heads_here = head_total // peers

    def send_tables():
        live = [counts[me[0] * heads_here + j] for j in range(heads_here)]
        wide_lists[...] = jnp.zeros_like(wide_lists)
        wide_lists[:heads_here, : lists.shape[1]] = lists[...]
        tables = pair_tables(wide_lists[...], lists.shape[1], live).astype(packed.dtype)
        for peer in range(peers):
            gone_tables[peer] = tables
        pltpu.make_async_copy(
            gone_tables, packed.at[:, pl.ds(heads_here * KINDS * rows, LIST_ROWS)], goes_sem
        ).start()

    weights = [counts[head] * head_total - head for head in range(head_total)]
    ranks = [jnp.int32(0)] * head_total
    for head in range(head_total):
        for other in range(head):
            ahead = (weights[other] > weights[head]).astype(jnp.int32)
            ranks[head] += ahead
            ranks[other] += 1 - ahead
    for head, rank in enumerate(ranks):
        order[rank] = head

    for head in range(head_total):
        if head == 0:
            send_tables()
        chunk, first = divmod(head, per_chunk)
        for kind in range(len(sources)):
            if first == 0:
                copies[chunk * len(sources) + kind].wait()
            goes[head, kind * rows : (kind + 1) * rows] = came[
                kind, :, head * head_dim : (head + 1) * head_dim
            ]
        peer, j = rank_to_place(ranks[head], peers)
        span = pl.ds(pl.multiple_of(j * KINDS * rows, rows), KINDS * rows)
        pltpu.make_async_copy(goes.at[head], packed.at[peer, span], goes_sem).start()
    pltpu.make_async_copy(packed, packed, goes_sem).wait()


def pack(me, counts, lists, queries, keys, values, peers):
    rows, columns = queries.shape
    head_total = counts.shape[0]
    head_dim = columns // head_total
    heads_here = head_total // peers
    parcel_rows = heads_here * KINDS * rows + LIST_ROWS
    return pl.pallas_call(
        pack_kernel,
        out_shape=(
            jax.ShapeDtypeStruct((peers, parcel_rows, head_dim), queries.dtype),
            jax.ShapeDtypeStruct((head_total,), jnp.int32),
        ),
        in_specs=[SMEM, SMEM, VMEM, ANY, ANY, ANY],
        out_specs=(ANY, SMEM),
        scratch_shapes=[
            pltpu.VMEM((KINDS, rows, columns), queries.dtype),
            pltpu.VMEM((head_total, KINDS * rows, head_dim), queries.dtype),
            pltpu.VMEM((PAIR_ROWS, head_dim), jnp.int32),
            pltpu.VMEM((peers, LIST_ROWS, head_dim), queries.dtype),
            pltpu.SemaphoreType.DMA((LOADS, KINDS)),
            pltpu.SemaphoreType.DMA,
        ],
        compiler_params=pltpu.CompilerParams(vmem_limit_bytes=60 * 1024 * 1024),
        name="pack",
    )(me, counts, lists, queries, keys, values)


def unpack_kernel(order, heads, out, staged, sems):
    peers, heads_here, rows, head_dim = heads.shape
    step = rows // CHUNKS
    copies = []
    for chunk in range(CHUNKS):
        span = pl.ds(chunk * step, step)
        for peer in range(peers):
            for j in range(heads_here):
                head = order[place_to_rank(peer, j, peers)]
                column = pl.multiple_of(head * head_dim, head_dim)
                staged[span, pl.ds(column, head_dim)] = heads[peer, j, span, :]
        copy = pltpu.make_async_copy(staged.at[span, :], out.at[span, :], sems.at[chunk])
        copy.start()
        copies.append(copy)
    for copy in copies:
        copy.wait()


def unpack(order, heads):
    peers, heads_here, rows, head_dim = heads.shape
    columns = peers * heads_here * head_dim
    return pl.pallas_call(
        unpack_kernel,
        out_shape=jax.ShapeDtypeStruct((rows, columns), heads.dtype),
        in_specs=[SMEM, VMEM],
        out_specs=ANY,
        scratch_shapes=[
            pltpu.VMEM((rows, columns), heads.dtype),
            pltpu.SemaphoreType.DMA((CHUNKS,)),
        ],
        compiler_params=pltpu.CompilerParams(vmem_limit_bytes=8 * 1024 * 1024),
        name="unpack",
    )(order, heads)


def heads_kernel(
    factor, me, order, parcels, out, values_t, held, held_max, acc, row_max, row_total, came_tables, tables, tables_sem
):
    nblocks, heads_here, rows, _ = out.shape
    peers = order.shape[0] // heads_here
    starts = []
    for j in range(heads_here):
        head = order[place_to_rank(me[0], j, peers)]
        sender = lax.div(head, heads_here)
        numbers = parcels[sender, pl.ds(heads_here * KINDS * rows, LIST_ROWS), :]
        came_tables[j * LIST_ROWS : (j + 1) * LIST_ROWS] = numbers.astype(jnp.float32).astype(jnp.int32)
        starts.append(j * LIST_ROWS + (head - sender * heads_here) * PAIR_ROWS)
    tables_copy = pltpu.make_async_copy(came_tables, tables, tables_sem)
    tables_copy.start()

    for j in range(heads_here):
        for a in range(nblocks):
            row = j * nblocks + a
            values_t[row] = parcels[a, tile_rows(j, 2, rows), :].T
            acc[row] = jnp.zeros_like(acc[row])
    row_max[...] = jnp.full_like(row_max, -jnp.inf)
    row_total[...] = jnp.zeros_like(row_total)

    tables_copy.wait()
    pairs = [tables[start + 3, 0] for start in starts]
    live = functools.reduce(lambda x, y: x + y, pairs)

    def locate(entry):
        entry = jnp.minimum(entry, live - 1)
        j = jnp.int32(0)
        start, place = starts[0], entry
        for later in range(1, heads_here):
            entry -= pairs[later - 1]
            j = jnp.where(entry >= 0, later, j)
            start = jnp.where(entry >= 0, starts[later], start)
            place = jnp.where(entry >= 0, entry, place)
        b, one, two = (tables[start + line, place] for line in range(3))
        return j, b, one, jnp.where(two == NONE, one, two), two != NONE

    def first_pass(index, carry):
        found = []
        for entry in [index * GROUP + lane for lane in range(GROUP)]:
            j, b, one, two, _ = locate(entry)
            both = jnp.concatenate(
                [parcels[one, tile_rows(j, 0, rows), :], parcels[two, tile_rows(j, 0, rows), :]], axis=0
            )
            scores = factor * lax.dot_general(
                parcels[b, tile_rows(j, 1, rows), :], both, NT, preferred_element_type=jnp.float32
            )
            block_max = jnp.max(scores, axis=0, keepdims=True)
            held[entry] = scores
            held_max[entry] = block_max
            found.append((j * nblocks + one, block_max[:, :rows]))
            found.append((j * nblocks + two, block_max[:, rows:]))
        for row, block_max in found:
            row_max[row] = jnp.maximum(row_max[row], block_max)
        return carry

    steps = (live + GROUP - 1) // GROUP
    lax.fori_loop(0, steps, first_pass, 0)

    def second_pass(index, carry):
        found = []
        for entry in [index * GROUP + lane for lane in range(GROUP)]:
            j, b, one, two, is_two = locate(entry)
            one, two = j * nblocks + one, j * nblocks + two
            block_max = held_max[entry]
            weights = jnp.exp2(held[entry] - block_max)
            is_live = entry < live
            share = jnp.concatenate(
                [
                    jnp.where(is_live, jnp.exp2(block_max[:, :rows] - row_max[one]), 0.0),
                    jnp.where(is_live & is_two, jnp.exp2(block_max[:, rows:] - row_max[two]), 0.0),
                ],
                axis=1,
            )
            total = share * jnp.sum(weights, axis=0, keepdims=True)
            product = share * lax.dot_general(
                values_t[j * nblocks + b],
                weights.astype(jnp.bfloat16),
                NN,
                preferred_element_type=jnp.float32,
            )
            found.append((one, total[:, :rows], product[:, :rows]))
            found.append((two, total[:, rows:], product[:, rows:]))
        for row, total, product in found:
            row_total[row] += total
            acc[row] += product
        return carry

    lax.fori_loop(0, steps, second_pass, 0)

    for j in range(heads_here):
        for a in range(nblocks):
            row = j * nblocks + a
            out[a, j] = (acc[row] * (1.0 / row_total[row])).T.astype(out.dtype)


def attend(me, order, parcels, list_len):
    nblocks, parcel_rows, head_dim = parcels.shape
    heads_here = order.shape[0] // nblocks
    rows = (parcel_rows - LIST_ROWS) // (heads_here * KINDS)
    factor = head_dim ** (-0.5) * math.log2(math.e)
    grid_rows = nblocks * heads_here
    slots = -(-heads_here * (list_len + 2 * nblocks) // (2 * GROUP)) * GROUP
    return pl.pallas_call(
        functools.partial(heads_kernel, factor),
        out_shape=jax.ShapeDtypeStruct((nblocks, heads_here, rows, head_dim), jnp.bfloat16),
        in_specs=[SMEM, SMEM, VMEM],
        out_specs=VMEM,
        scratch_shapes=[
            pltpu.VMEM((grid_rows, head_dim, rows), jnp.bfloat16),
            pltpu.VMEM((slots, rows, 2 * rows), jnp.float32),
            pltpu.VMEM((slots, 1, 2 * rows), jnp.float32),
            pltpu.VMEM((grid_rows, head_dim, rows), jnp.float32),
            pltpu.VMEM((grid_rows, 1, rows), jnp.float32),
            pltpu.VMEM((grid_rows, 1, rows), jnp.float32),
            pltpu.VMEM((heads_here * LIST_ROWS, head_dim), jnp.int32),
            pltpu.SMEM((heads_here * LIST_ROWS, head_dim), jnp.int32),
            pltpu.SemaphoreType.DMA,
        ],
        compiler_params=pltpu.CompilerParams(vmem_limit_bytes=36 * 1024 * 1024),
        name="attend",
    )(me, order, parcels)


def on_device(queries, key_vectors, value_vectors, keep_list, block_counts):
    peers = lax.axis_size("seq")
    me = lax.axis_index("seq").reshape(1)
    packed, order = pack(me, block_counts, keep_list, queries, key_vectors, value_vectors, peers)
    parcels = lax.all_to_all(packed, "seq", split_axis=0, concat_axis=0, tiled=True)
    attended = attend(me, order, parcels, keep_list.shape[1])
    returned = lax.all_to_all(attended, "seq", split_axis=0, concat_axis=0, tiled=True)
    return unpack(order, returned)


def solution(mesh):
    tokens = P(("batch", "seq"), None)
    return jax.shard_map(
        on_device,
        mesh=mesh,
        in_specs=(tokens, tokens, tokens, tokens, P("batch")),
        out_specs=tokens,
        check_vma=False,
    )
```

time: 134 us -> 132 us (0.985)
  blocking collectives: 32.5 us -> 118 us
  waiting for transfers between devices: 72.4 us -> 0 us
  starting transfers between devices: 11.8 us -> 0 us
  Pallas kernels: 17 us -> 13.3 us
    all_to_all x0 -> x1, blocking collectives: none -> 87 us  [on_device(): lax.all_to_all(packed, 'seq', split_axis=0, concat_axis=0, tiled=True)]
    all_to_all x1 -> x0, waiting for transfers between devices: 72.4 us -> none  [on_device(): lax.all_to_all(packed, 'seq', split_axis=0, concat_axis=0, tiled=True)]
    all_to_all x1 -> x0, starting transfers between devices: 11.8 us -> none  [on_device(): lax.all_to_all(packed, 'seq', split_axis=0, concat_axis=0, tiled=True)]
    pallas_call x1, Pallas kernels: 10.7 us -> 7.51 us  [attend(): pl.pallas_call(functools.partial(heads_kernel, factor), out_shape=jax.Sha...]
  transfers between devices with their start and end apart: 1 -> 0, of which waited for: 1 -> 0; matrix products, arithmetic and copies ran while one was open for 0% -> 0% of each run, Pallas kernels for 0% -> 0%
where the time goes in v4:
time: 132 us; the launch traced here: 131 us
  blocking collectives  118 us (89%)
  Pallas kernels  13.3 us (10%)
    all_to_all x1, blocking collectives, on_device(): lax.all_to_all(packed, 'seq', split_axis=0, concat_axis=0, tiled=True)  87 us
    all_to_all x1, blocking collectives, on_device(): lax.all_to_all(attended, 'seq', split_axis=0, concat_axis=0, tiled=True)  31.2 us
    pallas_call x1, Pallas kernels, attend(): pl.pallas_call(functools.partial(heads_kernel, factor), out_shape=jax.Sha...  7.51 us
    pallas_call x1, Pallas kernels, pack(): pl.pallas_call(pack_kernel, out_shape=(jax.ShapeDtypeStruct((peers, parce...  4.15 us

profile of v4, /device:TPU:1, one launch (start us, length us, event | category | flops | bytes accessed | tf_op | source)
XLA Modules:
  0.0 131.5 jit_solution(6746332596495308160)
XLA Ops:
  0.0 4.2 %pack.1 = (bf16[16,784,128]{2,1,0:T(8,128)(2,1)}, s32[32]{0:T(128)}) custom-call(s32[1]{0:T(128)} %bitcast.me, s32[32]{0:T(128)} %counts.1, s32[2,96]{1,0:T(2,128)} %lists.1, bf16[128,4096]{1,0:T(8,128)(2,1)} %queries.1, bf16[128,4096]{1,0:T(8,128)(2,1)} %keys.1, bf16[128,4096]{1,0:T(8,128)(2,1)} %values.1), custom_call_target="tpu_custom_call" | custom-call | tf_op jit(solution)/shard_map/pack/pallas_call | solution.py:148
  4.2 0.0 copy-start
  4.2 87.0 %all_to_all.10.parcels = bf16[16,784,128]{2,1,0:T(8,128)(2,1)S(1)} all-to-all(bf16[16,784,128]{2,1,0:T(8,128)(2,1)} %get-tuple-element.8), channel_id=1, replica_groups=mesh['seq'=16,'batch'=32] {'seq'}, dimensions={0} | all-to-all | bytes 6422528 | tf_op jit(solution)/shard_map/all_to_all | solution.py:334
  91.1 0.0 copy-done
  91.1 7.5 %attend.1 = bf16[16,2,128,128]{3,2,1,0:T(8,128)(2,1)S(1)} custom-call(s32[1]{0:T(128)} %bitcast.me, s32[32]{0:T(128)S(1)} %copy-done, bf16[16,784,128]{2,1,0:T(8,128)(2,1)S(1)} %all_to_all.10.parcels), custom_call_target="tpu_custom_call" | custom-call | tf_op jit(solution)/shard_map/attend/pallas_call | solution.py:309
  98.7 31.2 %all_to_all.11.heads = bf16[16,2,128,128]{3,2,1,0:T(8,128)(2,1)S(1)} all-to-all(bf16[16,2,128,128]{3,2,1,0:T(8,128)(2,1)S(1)} %attend.1), channel_id=1, replica_groups=mesh['seq'=16,'batch'=32] {'seq'}, dimensions={0} | all-to-all | bytes 2097152 | tf_op jit(solution)/shard_map/all_to_all | solution.py:336
  129.9 1.6 %unpack.1 = bf16[128,4096]{1,0:T(8,128)(2,1)} custom-call(s32[32]{0:T(128)S(1)} %copy-done, bf16[16,2,128,128]{3,2,1,0:T(8,128)(2,1)S(1)} %all_to_all.11.heads), custom_call_target="tpu_custom_call" | custom-call | tf_op jit(solution)/shard_map/unpack/pallas_call | solution.py:190
Async XLA Ops:
  4.2 87.0 %copy-start = (s32[32]{0:T(128)S(1)}, s32[32]{0:T(128)}, u32[]{:S(2)}) copy-start(s32[32]{0:T(128)} %get-tuple-element.7.order) | copy-start | bytes 388

commit v5 on v4

--- a/solution.py
+++ b/solution.py
@@ -14,7 +14,6 @@
 LOADS = 4
 KINDS = 3
 PAIR_ROWS = 8
-LIST_ROWS = 16
 NT = (((1,), (1,)), ((), ()))
 NN = (((1,), (0,)), ((), ()))
 VMEM = pl.BlockSpec(memory_space=pltpu.VMEM)
@@ -22,14 +21,20 @@
 ANY = pl.BlockSpec(memory_space=pl.ANY)
 
 
-def rank_to_place(rank, peers):
-    j = rank // peers
-    peer = rank - j * peers
-    return jnp.where(j % 2 == 0, peer, peers - 1 - peer), j
-
-
-def place_to_rank(peer, j, peers):
-    return j * peers + (peer if j % 2 == 0 else peers - 1 - peer)
+CORES = 2
+
+
+def rank_to_place(rank, heads_here):
+    j = lax.div(rank, CORES)
+    core = rank - j * CORES
+    return jnp.where(lax.rem(j, 2) == 0, core, CORES - 1 - core), j
+
+
+def place_to_slot(peer, j, heads_here):
+    chip = lax.div(peer, CORES)
+    core = peer - chip * CORES
+    rank = j * CORES + (core if j % 2 == 0 else CORES - 1 - core)
+    return chip * CORES * heads_here + rank
 
 
 def tile_rows(j, kind, rows):
@@ -82,9 +87,30 @@
     return jnp.concatenate(tables, axis=0)
 
 
-def pack_kernel(
-    me, counts, lists, queries, keys, values, packed, order, came, goes, wide_lists, gone_tables, came_sems, goes_sem
-):
+def tables_kernel(me, counts, order, lists, tables, wide_lists):
+    heads_here, list_len = lists.shape
+    live = [counts[me[0] * heads_here + j] for j in range(heads_here)]
+    wide_lists[...] = jnp.zeros_like(wide_lists)
+    wide_lists[:heads_here, :list_len] = lists[...]
+    tables[...] = pair_tables(wide_lists[...], list_len, live).astype(jnp.int32)
+
+
+def share_tables(me, counts, order, lists, peers):
+    heads_here = lists.shape[0]
+    width = 128
+    tables = pl.pallas_call(
+        tables_kernel,
+        out_shape=jax.ShapeDtypeStruct((heads_here * PAIR_ROWS, width), jnp.int32),
+        in_specs=[SMEM, SMEM, SMEM, VMEM],
+        out_specs=VMEM,
+        scratch_shapes=[pltpu.VMEM((PAIR_ROWS, width), jnp.int32)],
+        name="pair_tables",
+    )(me, counts, order, lists)
+    route = [(s, s ^ 1) for s in range(peers)]
+    return jnp.stack([tables, lax.ppermute(tables, "seq", route)])
+
+
+def pack_kernel(counts, queries, keys, values, packed, order, came, goes, came_sems, goes_sem):
     peers, _, head_dim = packed.shape
     head_total = counts.shape[0]
     rows = queries.shape[0]
@@ -101,31 +127,18 @@
             copies.append(copy)
 
     heads_here = head_total // peers
-
-    def send_tables():
-        live = [counts[me[0] * heads_here + j] for j in range(heads_here)]
-        wide_lists[...] = jnp.zeros_like(wide_lists)
-        wide_lists[:heads_here, : lists.shape[1]] = lists[...]
-        tables = pair_tables(wide_lists[...], lists.shape[1], live).astype(packed.dtype)
-        for peer in range(peers):
-            gone_tables[peer] = tables
-        pltpu.make_async_copy(
-            gone_tables, packed.at[:, pl.ds(heads_here * KINDS * rows, LIST_ROWS)], goes_sem
-        ).start()
-
+    shared = CORES * heads_here
     weights = [counts[head] * head_total - head for head in range(head_total)]
     ranks = [jnp.int32(0)] * head_total
     for head in range(head_total):
-        for other in range(head):
+        for other in range(head - head % shared, head):
             ahead = (weights[other] > weights[head]).astype(jnp.int32)
             ranks[head] += ahead
             ranks[other] += 1 - ahead
     for head, rank in enumerate(ranks):
-        order[rank] = head
+        order[head - head % shared + rank] = head
 
     for head in range(head_total):
-        if head == 0:
-            send_tables()
         chunk, first = divmod(head, per_chunk)
         for kind in range(len(sources)):
             if first == 0:
@@ -133,37 +146,35 @@
             goes[head, kind * rows : (kind + 1) * rows] = came[
                 kind, :, head * head_dim : (head + 1) * head_dim
             ]
-        peer, j = rank_to_place(ranks[head], peers)
+        core, j = rank_to_place(ranks[head], heads_here)
+        peer = head // shared * CORES + core
         span = pl.ds(pl.multiple_of(j * KINDS * rows, rows), KINDS * rows)
         pltpu.make_async_copy(goes.at[head], packed.at[peer, span], goes_sem).start()
     pltpu.make_async_copy(packed, packed, goes_sem).wait()
 
 
-def pack(me, counts, lists, queries, keys, values, peers):
+def pack(counts, queries, keys, values, peers):
     rows, columns = queries.shape
     head_total = counts.shape[0]
     head_dim = columns // head_total
     heads_here = head_total // peers
-    parcel_rows = heads_here * KINDS * rows + LIST_ROWS
     return pl.pallas_call(
         pack_kernel,
         out_shape=(
-            jax.ShapeDtypeStruct((peers, parcel_rows, head_dim), queries.dtype),
+            jax.ShapeDtypeStruct((peers, heads_here * KINDS * rows, head_dim), queries.dtype),
             jax.ShapeDtypeStruct((head_total,), jnp.int32),
         ),
-        in_specs=[SMEM, SMEM, VMEM, ANY, ANY, ANY],
+        in_specs=[SMEM, ANY, ANY, ANY],
         out_specs=(ANY, SMEM),
         scratch_shapes=[
             pltpu.VMEM((KINDS, rows, columns), queries.dtype),
             pltpu.VMEM((head_total, KINDS * rows, head_dim), queries.dtype),
-            pltpu.VMEM((PAIR_ROWS, head_dim), jnp.int32),
-            pltpu.VMEM((peers, LIST_ROWS, head_dim), queries.dtype),
             pltpu.SemaphoreType.DMA((LOADS, KINDS)),
             pltpu.SemaphoreType.DMA,
         ],
         compiler_params=pltpu.CompilerParams(vmem_limit_bytes=60 * 1024 * 1024),
         name="pack",
-    )(me, counts, lists, queries, keys, values)
+    )(counts, queries, keys, values)
 
 
 def unpack_kernel(order, heads, out, staged, sems):
@@ -174,7 +185,7 @@
         span = pl.ds(chunk * step, step)
         for peer in range(peers):
             for j in range(heads_here):
-                head = order[place_to_rank(peer, j, peers)]
+                head = order[place_to_slot(peer, j, heads_here)]
                 column = pl.multiple_of(head * head_dim, head_dim)
                 staged[span, pl.ds(column, head_dim)] = heads[peer, j, span, :]
         copy = pltpu.make_async_copy(staged.at[span, :], out.at[span, :], sems.at[chunk])
@@ -202,19 +213,22 @@
 
 
 def heads_kernel(
-    factor, me, order, parcels, out, values_t, held, held_max, acc, row_max, row_total, came_tables, tables, tables_sem
+    factor, me, order, parcels, all_tables, out, values_t, held, held_max, acc, row_max, row_total, tables, tables_sem
 ):
     nblocks, heads_here, rows, _ = out.shape
-    peers = order.shape[0] // heads_here
-    starts = []
+    starts, copies = [], []
+    height = all_tables.shape[1]
     for j in range(heads_here):
-        head = order[place_to_rank(me[0], j, peers)]
+        head = order[place_to_slot(me[0], j, heads_here)]
         sender = lax.div(head, heads_here)
-        numbers = parcels[sender, pl.ds(heads_here * KINDS * rows, LIST_ROWS), :]
-        came_tables[j * LIST_ROWS : (j + 1) * LIST_ROWS] = numbers.astype(jnp.float32).astype(jnp.int32)
-        starts.append(j * LIST_ROWS + (head - sender * heads_here) * PAIR_ROWS)
-    tables_copy = pltpu.make_async_copy(came_tables, tables, tables_sem)
-    tables_copy.start()
+        copy = pltpu.make_async_copy(
+            all_tables.at[lax.bitwise_xor(me[0], sender)],
+            tables.at[pl.ds(j * height, height)],
+            tables_sem.at[j],
+        )
+        copy.start()
+        copies.append(copy)
+        starts.append(j * height + (head - sender * heads_here) * PAIR_ROWS)
 
     for j in range(heads_here):
         for a in range(nblocks):
@@ -224,7 +238,8 @@
     row_max[...] = jnp.full_like(row_max, -jnp.inf)
     row_total[...] = jnp.zeros_like(row_total)
 
-    tables_copy.wait()
+    for copy in copies:
+        copy.wait()
     pairs = [tables[start + 3, 0] for start in starts]
     live = functools.reduce(lambda x, y: x + y, pairs)
 
@@ -299,17 +314,17 @@
             out[a, j] = (acc[row] * (1.0 / row_total[row])).T.astype(out.dtype)
 
 
-def attend(me, order, parcels, list_len):
+def attend(me, order, parcels, all_tables, list_len):
     nblocks, parcel_rows, head_dim = parcels.shape
     heads_here = order.shape[0] // nblocks
-    rows = (parcel_rows - LIST_ROWS) // (heads_here * KINDS)
+    rows = parcel_rows // (heads_here * KINDS)
     factor = head_dim ** (-0.5) * math.log2(math.e)
     grid_rows = nblocks * heads_here
     slots = -(-heads_here * (list_len + 2 * nblocks) // (2 * GROUP)) * GROUP
     return pl.pallas_call(
         functools.partial(heads_kernel, factor),
         out_shape=jax.ShapeDtypeStruct((nblocks, heads_here, rows, head_dim), jnp.bfloat16),
-        in_specs=[SMEM, SMEM, VMEM],
+        in_specs=[SMEM, SMEM, VMEM, ANY],
         out_specs=VMEM,
         scratch_shapes=[
             pltpu.VMEM((grid_rows, head_dim, rows), jnp.bfloat16),
@@ -318,21 +333,21 @@
             pltpu.VMEM((grid_rows, head_dim, rows), jnp.float32),
             pltpu.VMEM((grid_rows, 1, rows), jnp.float32),
             pltpu.VMEM((grid_rows, 1, rows), jnp.float32),
-            pltpu.VMEM((heads_here * LIST_ROWS, head_dim), jnp.int32),
-            pltpu.SMEM((heads_here * LIST_ROWS, head_dim), jnp.int32),
-            pltpu.SemaphoreType.DMA,
+            pltpu.SMEM((heads_here * all_tables.shape[1], all_tables.shape[2]), jnp.int32),
+            pltpu.SemaphoreType.DMA((heads_here,)),
         ],
         compiler_params=pltpu.CompilerParams(vmem_limit_bytes=36 * 1024 * 1024),
         name="attend",
-    )(me, order, parcels)
+    )(me, order, parcels, all_tables)
 
 
 def on_device(queries, key_vectors, value_vectors, keep_list, block_counts):
     peers = lax.axis_size("seq")
     me = lax.axis_index("seq").reshape(1)
-    packed, order = pack(me, block_counts, keep_list, queries, key_vectors, value_vectors, peers)
+    packed, order = pack(block_counts, queries, key_vectors, value_vectors, peers)
     parcels = lax.all_to_all(packed, "seq", split_axis=0, concat_axis=0, tiled=True)
-    attended = attend(me, order, parcels, keep_list.shape[1])
+    all_tables = share_tables(me, block_counts, order, keep_list, peers)
+    attended = attend(me, order, parcels, all_tables, keep_list.shape[1])
     returned = lax.all_to_all(attended, "seq", split_axis=0, concat_axis=0, tiled=True)
     return unpack(order, returned)
 

time: 132 us -> 131 us (level)
  blocking collectives: 118 us -> 35.9 us
  waiting for transfers between devices: 0 us -> 66.4 us
  starting transfers between devices: 0 us -> 13.8 us
    all_to_all x1 -> x0, blocking collectives: 87 us -> none  [on_device(): lax.all_to_all(packed, 'seq', split_axis=0, concat_axis=0, tiled=True)]
    all_to_all x0 -> x1, waiting for transfers between devices: none -> 65.1 us  [on_device(): lax.all_to_all(packed, 'seq', split_axis=0, concat_axis=0, tiled=True)]
    all_to_all x0 -> x1, starting transfers between devices: none -> 11.8 us  [on_device(): lax.all_to_all(packed, 'seq', split_axis=0, concat_axis=0, tiled=True)]
    all_to_all x1, blocking collectives: 31.2 us -> 35.9 us  [on_device(): lax.all_to_all(attended, 'seq', split_axis=0, concat_axis=0, tiled=True)]
    pallas_call x1, Pallas kernels: 7.51 us -> 5.01 us  [attend(): pl.pallas_call(functools.partial(heads_kernel, factor), out_shape=jax.Sha...]
    ppermute x0 -> x1, starting transfers between devices: none -> 2.01 us  [share_tables(): return jnp.stack([tables, lax.ppermute(tables, 'seq', route)])]
    pallas_call x1 -> x2, Pallas kernels: 4.15 us -> 5.96 us  [the longest x1 4.06 us: pack(): pl.pallas_call(pack_kernel, out_shape=(jax.ShapeDtypeStruct((peers, heads...]
  transfers between devices with their start and end apart: 0 -> 2, of which waited for: 0 -> 2; matrix products, arithmetic and copies ran while one was open for 0% -> 1% of each run, Pallas kernels for 0% -> 1%
where the time goes in v5:
time: 131 us; the launch traced here: 129 us
  waiting for transfers between devices  66.4 us (51%)
  blocking collectives  35.9 us (27%)
  starting transfers between devices  13.8 us (11%)
  Pallas kernels  12.6 us (10%)
    all_to_all x1, waiting for transfers between devices, on_device(): lax.all_to_all(packed, 'seq', split_axis=0, concat_axis=0, tiled=True)  65.1 us
    all_to_all x1, blocking collectives, on_device(): lax.all_to_all(attended, 'seq', split_axis=0, concat_axis=0, tiled=True)  35.9 us
    all_to_all x1, starting transfers between devices, on_device(): lax.all_to_all(packed, 'seq', split_axis=0, concat_axis=0, tiled=True)  11.8 us
    pallas_call x1, Pallas kernels, attend(): pl.pallas_call(functools.partial(heads_kernel, factor), out_shape=jax.Sha...  5.01 us
    pallas_call x1, Pallas kernels, pack(): pl.pallas_call(pack_kernel, out_shape=(jax.ShapeDtypeStruct((peers, heads...  4.06 us
  transfers between devices with their start and end apart: 2, of which 2 were waited for; matrix products, arithmetic and copies ran while one was open for 1% of the time, Pallas kernels for 1%

profile of v5, /device:TPU:1, one launch (start us, length us, event | category | flops | bytes accessed | tf_op | source)
XLA Modules:
  0.0 129.4 jit_solution(12101589419401762705)
XLA Ops:
  0.0 4.1 %pack.1 = (bf16[16,768,128]{2,1,0:T(8,128)(2,1)}, s32[32]{0:T(128)}) custom-call(s32[32]{0:T(128)} %counts.3, bf16[128,4096]{1,0:T(8,128)(2,1)} %queries.1, bf16[128,4096]{1,0:T(8,128)(2,1)} %keys.1, bf16[128,4096]{1,0:T(8,128)(2,1)} %values.1), custom_call_target="tpu_custom_call" | custom-call | tf_op jit(solution)/shard_map/pack/pallas_call | solution.py:161
  4.1 0.0 copy-start
  4.1 11.8 %all-to-all-start = ((bf16[16,768,128]{2,1,0:T(8,128)(2,1)}), bf16[16,768,128]{2,1,0:T(8,128)(2,1)S(1)}, u32[]{:S(2)}, u32[]{:S(2)}) async-start(bf16[16,768,128]{2,1,0:T(8,128)(2,1)} %get-tuple-element.8), calls=%async_computation | async-start | bytes 6291456 | tf_op jit(solution)/shard_map/all_to_all | solution.py:348
  15.9 1.9 %pair_tables.1 = s32[16,128]{1,0:T(8,128)} custom-call(s32[1]{0:T(128)} %bitcast.me, s32[32]{0:T(128)} %counts.3, s32[32]{0:T(128)} %get-tuple-element.7.order, s32[2,96]{1,0:T(2,128)} %lists.1), custom_call_target="tpu_custom_call" | custom-call | tf_op jit(solution)/shard_map/pair_tables/pallas_call | solution.py:101
  17.8 2.0 %collective-permute-start = (s32[16,128]{1,0:T(8,128)}, s32[16,128]{1,0:T(8,128)S(1)}, u32[]{:S(2)}, u32[]{:S(2)}) collective-permute-start(s32[16,128]{1,0:T(8,128)} %pair_tables.1), channel_id=1, source_target_pairs={{0,32},{32,0},{64,96},{96,64},{128,160},{160,128},{192,224},{224,1... | collective-permute-start | bytes 24584 | tf_op jit(solution)/shard_map/ppermute | solution.py:110
  19.8 1.3 collective-permute-done
  21.1 0.7 pad_add_fusion.all_tables
  21.8 65.1 %all-to-all-done.parcels = bf16[16,768,128]{2,1,0:T(8,128)(2,1)S(1)} async-done(((bf16[16,768,128]{2,1,0:T(8,128)(2,1)}), bf16[16,768,128]{2,1,0:T(8,128)(2,1)S(1)}, u32[]{:S(2)}, u32[]{:S(2)}) %all-to-all-start) | async-done | bytes 3145760 | tf_op jit(solution)/shard_map/all_to_all | solution.py:348
  86.9 0.0 copy-done
  86.9 5.0 %attend.1 = bf16[16,2,128,128]{3,2,1,0:T(8,128)(2,1)S(1)} custom-call(s32[1]{0:T(128)} %bitcast.me, s32[32]{0:T(128)S(1)} %copy-done, bf16[16,768,128]{2,1,0:T(8,128)(2,1)S(1)} %all-to-all-done.parcels, s32[2,16,128]{2,1,0:T(8,128)S(1)} %pad_add_fusion.all_tables), custom_call_target="tpu_custom_call" | custom-call | tf_op jit(solution)/shard_map/attend/pallas_call | solution.py:324
  91.9 35.9 %all_to_all.10.heads = bf16[16,2,128,128]{3,2,1,0:T(8,128)(2,1)S(1)} all-to-all(bf16[16,2,128,128]{3,2,1,0:T(8,128)(2,1)S(1)} %attend.1), channel_id=1, replica_groups=mesh['seq'=16,'batch'=32] {'seq'}, dimensions={0} | all-to-all | bytes 2097152 | tf_op jit(solution)/shard_map/all_to_all | solution.py:351
  127.8 1.6 %unpack.1 = bf16[128,4096]{1,0:T(8,128)(2,1)} custom-call(s32[32]{0:T(128)S(1)} %copy-done, bf16[16,2,128,128]{3,2,1,0:T(8,128)(2,1)S(1)} %all_to_all.10.heads), custom_call_target="tpu_custom_call" | custom-call | tf_op jit(solution)/shard_map/unpack/pallas_call | solution.py:201
Async XLA Ops:
  4.1 82.8 %copy-start = (s32[32]{0:T(128)S(1)}, s32[32]{0:T(128)}, u32[]{:S(2)}) copy-start(s32[32]{0:T(128)} %get-tuple-element.7.order) | copy-start | bytes 388
  4.1 82.8 %all-to-all-start = ((bf16[16,768,128]{2,1,0:T(8,128)(2,1)}), bf16[16,768,128]{2,1,0:T(8,128)(2,1)S(1)}, u32[]{:S(2)}, u32[]{:S(2)}) async-start(bf16[16,768,128]{2,1,0:T(8,128)(2,1)} %get-tuple-element.8), calls=%async_computation | async-start | bytes 6291456 | tf_op jit(solution)/shard_map/all_to_all | solution.py:348
  17.8 3.3 %collective-permute-start = (s32[16,128]{1,0:T(8,128)}, s32[16,128]{1,0:T(8,128)S(1)}, u32[]{:S(2)}, u32[]{:S(2)}) collective-permute-start(s32[16,128]{1,0:T(8,128)} %pair_tables.1), channel_id=1, source_target_pairs={{0,32},{32,0},{64,96},{96,64},{128,160},{160,128},{192,224},{224,1... | collective-permute-start | bytes 24584 | tf_op jit(solution)/shard_map/ppermute | solution.py:110

commit v6 on v5

--- a/solution.py
+++ b/solution.py
@@ -22,6 +22,7 @@
 
 
 CORES = 2
+ORDER_WIDTH = 128
 
 
 def rank_to_place(rank, heads_here):
@@ -95,22 +96,32 @@
     tables[...] = pair_tables(wide_lists[...], list_len, live).astype(jnp.int32)
 
 
-def share_tables(me, counts, order, lists, peers):
+def own_tables(me, counts, order, lists, peers):
     heads_here = lists.shape[0]
     width = 128
-    tables = pl.pallas_call(
+    shape = jax.ShapeDtypeStruct((heads_here * PAIR_ROWS, width), jnp.int32)
+    ours = pl.pallas_call(
         tables_kernel,
-        out_shape=jax.ShapeDtypeStruct((heads_here * PAIR_ROWS, width), jnp.int32),
+        out_shape=shape,
         in_specs=[SMEM, SMEM, SMEM, VMEM],
         out_specs=VMEM,
         scratch_shapes=[pltpu.VMEM((PAIR_ROWS, width), jnp.int32)],
         name="pair_tables",
     )(me, counts, order, lists)
-    route = [(s, s ^ 1) for s in range(peers)]
-    return jnp.stack([tables, lax.ppermute(tables, "seq", route)])
-
-
-def pack_kernel(counts, queries, keys, values, packed, order, came, goes, came_sems, goes_sem):
+    theirs = lax.ppermute(ours, "seq", [(s, s ^ 1) for s in range(peers)])
+    tables = jnp.concatenate([ours, theirs]).reshape(CORES * heads_here, PAIR_ROWS, width)
+    picked = []
+    for j in range(heads_here):
+        head = order[0, place_to_slot(me[0], j, heads_here)]
+        sender = lax.div(head, heads_here)
+        at = head - sender * heads_here + heads_here * (sender != me[0]).astype(jnp.int32)
+        picked.append(lax.dynamic_index_in_dim(tables, at, keepdims=False))
+    return jnp.concatenate(picked)
+
+
+def pack_kernel(
+    counts, queries, keys, values, packed, order_out, came, goes, order, came_sems, goes_sem, order_sem
+):
     peers, _, head_dim = packed.shape
     head_total = counts.shape[0]
     rows = queries.shape[0]
@@ -136,7 +147,9 @@
             ranks[head] += ahead
             ranks[other] += 1 - ahead
     for head, rank in enumerate(ranks):
-        order[head - head % shared + rank] = head
+        order[0, head - head % shared + rank] = head
+    order_copy = pltpu.make_async_copy(order, order_out, order_sem)
+    order_copy.start()
 
     for head in range(head_total):
         chunk, first = divmod(head, per_chunk)
@@ -150,6 +163,7 @@
         peer = head // shared * CORES + core
         span = pl.ds(pl.multiple_of(j * KINDS * rows, rows), KINDS * rows)
         pltpu.make_async_copy(goes.at[head], packed.at[peer, span], goes_sem).start()
+    order_copy.wait()
     pltpu.make_async_copy(packed, packed, goes_sem).wait()
 
 
@@ -162,14 +176,16 @@
         pack_kernel,
         out_shape=(
             jax.ShapeDtypeStruct((peers, heads_here * KINDS * rows, head_dim), queries.dtype),
-            jax.ShapeDtypeStruct((head_total,), jnp.int32),
+            jax.ShapeDtypeStruct((1, ORDER_WIDTH), jnp.int32),
         ),
         in_specs=[SMEM, ANY, ANY, ANY],
-        out_specs=(ANY, SMEM),
+        out_specs=(ANY, ANY),
         scratch_shapes=[
             pltpu.VMEM((KINDS, rows, columns), queries.dtype),
             pltpu.VMEM((head_total, KINDS * rows, head_dim), queries.dtype),
+            pltpu.SMEM((1, ORDER_WIDTH), jnp.int32),
             pltpu.SemaphoreType.DMA((LOADS, KINDS)),
+            pltpu.SemaphoreType.DMA,
             pltpu.SemaphoreType.DMA,
         ],
         compiler_params=pltpu.CompilerParams(vmem_limit_bytes=60 * 1024 * 1024),
@@ -185,7 +201,7 @@
         span = pl.ds(chunk * step, step)
         for peer in range(peers):
             for j in range(heads_here):
-                head = order[place_to_slot(peer, j, heads_here)]
+                head = order[0, place_to_slot(peer, j, heads_here)]
                 column = pl.multiple_of(head * head_dim, head_dim)
                 staged[span, pl.ds(column, head_dim)] = heads[peer, j, span, :]
         copy = pltpu.make_async_copy(staged.at[span, :], out.at[span, :], sems.at[chunk])
@@ -212,24 +228,11 @@
     )(order, heads)
 
 
-def heads_kernel(
-    factor, me, order, parcels, all_tables, out, values_t, held, held_max, acc, row_max, row_total, tables, tables_sem
-):
+def heads_kernel(factor, tables_in, parcels, out, values_t, held, held_max, tables, tables_sem, acc, row_max, row_total):
     nblocks, heads_here, rows, _ = out.shape
-    starts, copies = [], []
-    height = all_tables.shape[1]
-    for j in range(heads_here):
-        head = order[place_to_slot(me[0], j, heads_here)]
-        sender = lax.div(head, heads_here)
-        copy = pltpu.make_async_copy(
-            all_tables.at[lax.bitwise_xor(me[0], sender)],
-            tables.at[pl.ds(j * height, height)],
-            tables_sem.at[j],
-        )
-        copy.start()
-        copies.append(copy)
-        starts.append(j * height + (head - sender * heads_here) * PAIR_ROWS)
-
+    starts = [j * PAIR_ROWS for j in range(heads_here)]
+    tables_copy = pltpu.make_async_copy(tables_in, tables, tables_sem)
+    tables_copy.start()
     for j in range(heads_here):
         for a in range(nblocks):
             row = j * nblocks + a
@@ -238,8 +241,7 @@
     row_max[...] = jnp.full_like(row_max, -jnp.inf)
     row_total[...] = jnp.zeros_like(row_total)
 
-    for copy in copies:
-        copy.wait()
+    tables_copy.wait()
     pairs = [tables[start + 3, 0] for start in starts]
     live = functools.reduce(lambda x, y: x + y, pairs)
 
@@ -314,9 +316,9 @@
             out[a, j] = (acc[row] * (1.0 / row_total[row])).T.astype(out.dtype)
 
 
-def attend(me, order, parcels, all_tables, list_len):
+def attend(tables, parcels, list_len):
     nblocks, parcel_rows, head_dim = parcels.shape
-    heads_here = order.shape[0] // nblocks
+    heads_here = tables.shape[0] // PAIR_ROWS
     rows = parcel_rows // (heads_here * KINDS)
     factor = head_dim ** (-0.5) * math.log2(math.e)
     grid_rows = nblocks * heads_here
@@ -324,21 +326,21 @@
     return pl.pallas_call(
         functools.partial(heads_kernel, factor),
         out_shape=jax.ShapeDtypeStruct((nblocks, heads_here, rows, head_dim), jnp.bfloat16),
-        in_specs=[SMEM, SMEM, VMEM, ANY],
+        in_specs=[ANY, VMEM],
         out_specs=VMEM,
         scratch_shapes=[
             pltpu.VMEM((grid_rows, head_dim, rows), jnp.bfloat16),
             pltpu.VMEM((slots, rows, 2 * rows), jnp.float32),
             pltpu.VMEM((slots, 1, 2 * rows), jnp.float32),
+            pltpu.SMEM(tables.shape, jnp.int32),
+            pltpu.SemaphoreType.DMA,
             pltpu.VMEM((grid_rows, head_dim, rows), jnp.float32),
             pltpu.VMEM((grid_rows, 1, rows), jnp.float32),
             pltpu.VMEM((grid_rows, 1, rows), jnp.float32),
-            pltpu.SMEM((heads_here * all_tables.shape[1], all_tables.shape[2]), jnp.int32),
-            pltpu.SemaphoreType.DMA((heads_here,)),
         ],
         compiler_params=pltpu.CompilerParams(vmem_limit_bytes=36 * 1024 * 1024),
         name="attend",
-    )(me, order, parcels, all_tables)
+    )(tables, parcels)
 
 
 def on_device(queries, key_vectors, value_vectors, keep_list, block_counts):
@@ -346,8 +348,8 @@
     me = lax.axis_index("seq").reshape(1)
     packed, order = pack(block_counts, queries, key_vectors, value_vectors, peers)
     parcels = lax.all_to_all(packed, "seq", split_axis=0, concat_axis=0, tiled=True)
-    all_tables = share_tables(me, block_counts, order, keep_list, peers)
-    attended = attend(me, order, parcels, all_tables, keep_list.shape[1])
+    tables = own_tables(me, block_counts, order, keep_list, peers)
+    attended = attend(tables, parcels, keep_list.shape[1])
     returned = lax.all_to_all(attended, "seq", split_axis=0, concat_axis=0, tiled=True)
     return unpack(order, returned)
 

time: 131 us -> 129 us (0.985)
  waiting for transfers between devices: 66.4 us -> 60.9 us
  between operations: 0.04 us -> 4.89 us
    all_to_all x1, waiting for transfers between devices: 65.1 us -> 60.9 us  [on_device(): lax.all_to_all(packed, 'seq', split_axis=0, concat_axis=0, tiled=True)]
  transfers between devices with their start and end apart: 2 -> 2, of which waited for: 2 -> 1; matrix products, arithmetic and copies ran while one was open for 1% -> 1% of each run, Pallas kernels for 1% -> 1%
where the time goes in v6:
time: 129 us; the launch traced here: 128 us
  waiting for transfers between devices  60.9 us (47%)
  blocking collectives  35.9 us (28%)
  starting transfers between devices  13.8 us (11%)
  Pallas kernels  11.5 us (9%)
  between operations  4.89 us (4%)
    all_to_all x1, waiting for transfers between devices, on_device(): lax.all_to_all(packed, 'seq', split_axis=0, concat_axis=0, tiled=True)  60.9 us
    all_to_all x1, blocking collectives, on_device(): lax.all_to_all(attended, 'seq', split_axis=0, concat_axis=0, tiled=True)  35.9 us
    all_to_all x1, starting transfers between devices, on_device(): lax.all_to_all(packed, 'seq', split_axis=0, concat_axis=0, tiled=True)  11.8 us
    pallas_call x1, Pallas kernels, attend(): pl.pallas_call(functools.partial(heads_kernel, factor), out_shape=jax.Sha...  4.42 us
    pallas_call x1, Pallas kernels, pack(): pl.pallas_call(pack_kernel, out_shape=(jax.ShapeDtypeStruct((peers, heads...  3.55 us
  transfers between devices with their start and end apart: 2, of which 1 were waited for; matrix products, arithmetic and copies ran while one was open for 1% of the time, Pallas kernels for 1%

profile of v6, /device:TPU:1, one launch (start us, length us, event | category | flops | bytes accessed | tf_op | source)
XLA Modules:
  0.0 128.4 jit_solution(18202920068758829335)
XLA Ops:
  0.0 3.6 %pack.1 = (bf16[16,768,128]{2,1,0:T(8,128)(2,1)}, s32[1,128]{1,0:T(1,128)}) custom-call(s32[32]{0:T(128)} %counts.3, bf16[128,4096]{1,0:T(8,128)(2,1)} %queries.1, bf16[128,4096]{1,0:T(8,128)(2,1)} %keys.1, bf16[128,4096]{1,0:T(8,128)(2,1)} %values.1), custom_call_target="tpu_custom_call" | custom-call | tf_op jit(solution)/shard_map/pack/pallas_call | solution.py:175
  3.6 0.0 copy-start
  3.6 11.8 %all-to-all-start = ((bf16[16,768,128]{2,1,0:T(8,128)(2,1)}), bf16[16,768,128]{2,1,0:T(8,128)(2,1)S(1)}, u32[]{:S(2)}, u32[]{:S(2)}) async-start(bf16[16,768,128]{2,1,0:T(8,128)(2,1)} %get-tuple-element.8), calls=%async_computation | async-start | bytes 6291456 | tf_op jit(solution)/shard_map/all_to_all | solution.py:350
  15.4 1.9 %pair_tables.1 = s32[16,128]{1,0:T(8,128)} custom-call(s32[1]{0:T(128)} %bitcast.me, s32[32]{0:T(128)} %counts.3, s32[1,128]{1,0:T(1,128)} %get-tuple-element.7.order, s32[2,96]{1,0:T(2,128)} %lists.1), custom_call_target="tpu_custom_call" | custom-call | tf_op jit(solution)/shard_map/pair_tables/pallas_call | solution.py:103
  17.3 2.0 %collective-permute-start = (s32[16,128]{1,0:T(8,128)}, s32[16,128]{1,0:T(8,128)S(1)}, u32[]{:S(2)}, u32[]{:S(2)}) collective-permute-start(s32[16,128]{1,0:T(8,128)} %pair_tables.1), channel_id=1, source_target_pairs={{0,32},{32,0},{64,96},{96,64},{128,160},{160,128},{192,224},{224,1... | collective-permute-start | bytes 24584 | tf_op jit(solution)/shard_map/ppermute | solution.py:111
  19.3 0.0 copy-done
  19.4 0.6 constant_dynamic-slice_fusion.1
  24.8 0.0 collective-permute-done
  24.8 0.7 add_bitcast_fusion
  25.5 60.9 %all-to-all-done.parcels = bf16[16,768,128]{2,1,0:T(8,128)(2,1)S(1)} async-done(((bf16[16,768,128]{2,1,0:T(8,128)(2,1)}), bf16[16,768,128]{2,1,0:T(8,128)(2,1)S(1)}, u32[]{:S(2)}, u32[]{:S(2)}) %all-to-all-start) | async-done | bytes 3145760 | tf_op jit(solution)/shard_map/all_to_all | solution.py:350
  86.4 4.4 %attend.1 = bf16[16,2,128,128]{3,2,1,0:T(8,128)(2,1)S(1)} custom-call(s32[16,128]{1,0:T(8,128)S(1)} %pad_add_fusion.tables_in, bf16[16,768,128]{2,1,0:T(8,128)(2,1)S(1)} %all-to-all-done.parcels), custom_call_target="tpu_custom_call" | custom-call | tf_op jit(solution)/shard_map/attend/pallas_call | solution.py:326
  90.8 35.9 %all_to_all.10.heads = bf16[16,2,128,128]{3,2,1,0:T(8,128)(2,1)S(1)} all-to-all(bf16[16,2,128,128]{3,2,1,0:T(8,128)(2,1)S(1)} %attend.1), channel_id=1, replica_groups=mesh['seq'=16,'batch'=32] {'seq'}, dimensions={0} | all-to-all | bytes 2097152 | tf_op jit(solution)/shard_map/all_to_all | solution.py:353
  126.8 1.6 %unpack.1 = bf16[128,4096]{1,0:T(8,128)(2,1)} custom-call(s32[1,128]{1,0:T(1,128)S(1)} %copy-done, bf16[16,2,128,128]{3,2,1,0:T(8,128)(2,1)S(1)} %all_to_all.10.heads), custom_call_target="tpu_custom_call" | custom-call | tf_op jit(solution)/shard_map/unpack/pallas_call | solution.py:217
  (2 shorter events, 0.0 us)
Async XLA Ops:
  3.6 15.8 %copy-start = (s32[1,128]{1,0:T(1,128)S(1)}, s32[1,128]{1,0:T(1,128)}, u32[]{:S(2)}) copy-start(s32[1,128]{1,0:T(1,128)} %get-tuple-element.7.order) | copy-start | bytes 1540
  3.6 82.8 %all-to-all-start = ((bf16[16,768,128]{2,1,0:T(8,128)(2,1)}), bf16[16,768,128]{2,1,0:T(8,128)(2,1)S(1)}, u32[]{:S(2)}, u32[]{:S(2)}) async-start(bf16[16,768,128]{2,1,0:T(8,128)(2,1)} %get-tuple-element.8), calls=%async_computation | async-start | bytes 6291456 | tf_op jit(solution)/shard_map/all_to_all | solution.py:350
  17.3 7.5 %collective-permute-start = (s32[16,128]{1,0:T(8,128)}, s32[16,128]{1,0:T(8,128)S(1)}, u32[]{:S(2)}, u32[]{:S(2)}) collective-permute-start(s32[16,128]{1,0:T(8,128)} %pair_tables.1), channel_id=1, source_target_pairs={{0,32},{32,0},{64,96},{96,64},{128,160},{160,128},{192,224},{224,1... | collective-permute-start | bytes 24584 | tf_op jit(solution)/shard_map/ppermute | solution.py:111

commit v7 on v6

--- a/solution.py
+++ b/solution.py
@@ -120,13 +120,15 @@
 
 
 def pack_kernel(
-    counts, queries, keys, values, packed, order_out, came, goes, order, came_sems, goes_sem, order_sem
+    counts_in, queries, keys, values, packed, order_out, came, goes, counts, order, came_sems, goes_sem, small_sems
 ):
     peers, _, head_dim = packed.shape
     head_total = counts.shape[0]
     rows = queries.shape[0]
     per_chunk = head_total // LOADS
     sources = (queries, keys, values)
+    counts_copy = pltpu.make_async_copy(counts_in, counts, small_sems.at[0])
+    counts_copy.start()
     copies = []
     for chunk in range(LOADS):
         span = pl.ds(chunk * per_chunk * head_dim, per_chunk * head_dim)
@@ -139,6 +141,7 @@
 
     heads_here = head_total // peers
     shared = CORES * heads_here
+    counts_copy.wait()
     weights = [counts[head] * head_total - head for head in range(head_total)]
     ranks = [jnp.int32(0)] * head_total
     for head in range(head_total):
@@ -148,7 +151,7 @@
             ranks[other] += 1 - ahead
     for head, rank in enumerate(ranks):
         order[0, head - head % shared + rank] = head
-    order_copy = pltpu.make_async_copy(order, order_out, order_sem)
+    order_copy = pltpu.make_async_copy(order, order_out, small_sems.at[1])
     order_copy.start()
 
     for head in range(head_total):
@@ -178,15 +181,16 @@
             jax.ShapeDtypeStruct((peers, heads_here * KINDS * rows, head_dim), queries.dtype),
             jax.ShapeDtypeStruct((1, ORDER_WIDTH), jnp.int32),
         ),
-        in_specs=[SMEM, ANY, ANY, ANY],
+        in_specs=[ANY, ANY, ANY, ANY],
         out_specs=(ANY, ANY),
         scratch_shapes=[
             pltpu.VMEM((KINDS, rows, columns), queries.dtype),
             pltpu.VMEM((head_total, KINDS * rows, head_dim), queries.dtype),
+            pltpu.SMEM((head_total,), jnp.int32),
             pltpu.SMEM((1, ORDER_WIDTH), jnp.int32),
             pltpu.SemaphoreType.DMA((LOADS, KINDS)),
             pltpu.SemaphoreType.DMA,
-            pltpu.SemaphoreType.DMA,
+            pltpu.SemaphoreType.DMA((2,)),
         ],
         compiler_params=pltpu.CompilerParams(vmem_limit_bytes=60 * 1024 * 1024),
         name="pack",

time: 129 us -> 128 us (level)
  no operation moved by 1% of the time
where the time goes in v7:
time: 128 us
  waiting for transfers between devices  60.9 us (48%)
  blocking collectives  35.9 us (28%)
  starting transfers between devices  13.8 us (11%)
  Pallas kernels  10.8 us (8%)
  between operations  4.89 us (4%)
    all_to_all x1, waiting for transfers between devices, on_device(): lax.all_to_all(packed, 'seq', split_axis=0, concat_axis=0, tiled=True)  60.9 us
    all_to_all x1, blocking collectives, on_device(): lax.all_to_all(attended, 'seq', split_axis=0, concat_axis=0, tiled=True)  35.9 us
    all_to_all x1, starting transfers between devices, on_device(): lax.all_to_all(packed, 'seq', split_axis=0, concat_axis=0, tiled=True)  11.8 us
    pallas_call x1, Pallas kernels, attend(): pl.pallas_call(functools.partial(heads_kernel, factor), out_shape=jax.Sha...  4.37 us
    pallas_call x1, Pallas kernels, pack(): pl.pallas_call(pack_kernel, out_shape=(jax.ShapeDtypeStruct((peers, heads...  2.91 us
  transfers between devices with their start and end apart: 2, of which 1 were waited for; matrix products, arithmetic and copies ran while one was open for 1% of the time, Pallas kernels for 1%

profile of v7, /device:TPU:1, one launch (start us, length us, event | category | flops | bytes accessed | tf_op | source)
XLA Modules:
  0.0 127.6 jit_solution(13102484219782998272)
XLA Ops:
  0.0 2.9 %pack.1 = (bf16[16,768,128]{2,1,0:T(8,128)(2,1)}, s32[1,128]{1,0:T(1,128)}) custom-call(s32[32]{0:T(128)} %counts.1, bf16[128,4096]{1,0:T(8,128)(2,1)} %queries.1, bf16[128,4096]{1,0:T(8,128)(2,1)} %keys.1, bf16[128,4096]{1,0:T(8,128)(2,1)} %values.1), custom_call_target="tpu_custom_call" | custom-call | tf_op jit(solution)/shard_map/pack/pallas_call | solution.py:178
  2.9 0.0 copy-start
  2.9 11.8 %all-to-all-start = ((bf16[16,768,128]{2,1,0:T(8,128)(2,1)}), bf16[16,768,128]{2,1,0:T(8,128)(2,1)S(1)}, u32[]{:S(2)}, u32[]{:S(2)}) async-start(bf16[16,768,128]{2,1,0:T(8,128)(2,1)} %get-tuple-element.8), calls=%async_computation | async-start | bytes 6291456 | tf_op jit(solution)/shard_map/all_to_all | solution.py:354
  14.8 1.9 %pair_tables.1 = s32[16,128]{1,0:T(8,128)} custom-call(s32[1]{0:T(128)} %bitcast.me, s32[32]{0:T(128)} %counts.1, s32[1,128]{1,0:T(1,128)} %get-tuple-element.7.order, s32[2,96]{1,0:T(2,128)} %lists.1), custom_call_target="tpu_custom_call" | custom-call | tf_op jit(solution)/shard_map/pair_tables/pallas_call | solution.py:103
  16.7 2.0 %collective-permute-start = (s32[16,128]{1,0:T(8,128)}, s32[16,128]{1,0:T(8,128)S(1)}, u32[]{:S(2)}, u32[]{:S(2)}) collective-permute-start(s32[16,128]{1,0:T(8,128)} %pair_tables.1), channel_id=1, source_target_pairs={{0,32},{32,0},{64,96},{96,64},{128,160},{160,128},{192,224},{224,1... | collective-permute-start | bytes 24584 | tf_op jit(solution)/shard_map/ppermute | solution.py:111
  18.7 0.0 copy-done
  18.7 0.6 constant_dynamic-slice_fusion.1
  24.1 0.0 collective-permute-done
  24.2 0.7 add_bitcast_fusion
  24.9 60.9 %all-to-all-done.parcels = bf16[16,768,128]{2,1,0:T(8,128)(2,1)S(1)} async-done(((bf16[16,768,128]{2,1,0:T(8,128)(2,1)}), bf16[16,768,128]{2,1,0:T(8,128)(2,1)S(1)}, u32[]{:S(2)}, u32[]{:S(2)}) %all-to-all-start) | async-done | bytes 3145760 | tf_op jit(solution)/shard_map/all_to_all | solution.py:354
  85.8 4.4 %attend.1 = bf16[16,2,128,128]{3,2,1,0:T(8,128)(2,1)S(1)} custom-call(s32[16,128]{1,0:T(8,128)S(1)} %pad_add_fusion.tables_in, bf16[16,768,128]{2,1,0:T(8,128)(2,1)S(1)} %all-to-all-done.parcels), custom_call_target="tpu_custom_call" | custom-call | tf_op jit(solution)/shard_map/attend/pallas_call | solution.py:330
  90.1 35.9 %all_to_all.10.heads = bf16[16,2,128,128]{3,2,1,0:T(8,128)(2,1)S(1)} all-to-all(bf16[16,2,128,128]{3,2,1,0:T(8,128)(2,1)S(1)} %attend.1), channel_id=1, replica_groups=mesh['seq'=16,'batch'=32] {'seq'}, dimensions={0} | all-to-all | bytes 2097152 | tf_op jit(solution)/shard_map/all_to_all | solution.py:357
  126.0 1.6 %unpack.1 = bf16[128,4096]{1,0:T(8,128)(2,1)} custom-call(s32[1,128]{1,0:T(1,128)S(1)} %copy-done, bf16[16,2,128,128]{3,2,1,0:T(8,128)(2,1)S(1)} %all_to_all.10.heads), custom_call_target="tpu_custom_call" | custom-call | tf_op jit(solution)/shard_map/unpack/pallas_call | solution.py:221
  (2 shorter events, 0.0 us)
Async XLA Ops:
  2.9 15.8 %copy-start = (s32[1,128]{1,0:T(1,128)S(1)}, s32[1,128]{1,0:T(1,128)}, u32[]{:S(2)}) copy-start(s32[1,128]{1,0:T(1,128)} %get-tuple-element.7.order) | copy-start | bytes 1540
  2.9 82.8 %all-to-all-start = ((bf16[16,768,128]{2,1,0:T(8,128)(2,1)}), bf16[16,768,128]{2,1,0:T(8,128)(2,1)S(1)}, u32[]{:S(2)}, u32[]{:S(2)}) async-start(bf16[16,768,128]{2,1,0:T(8,128)(2,1)} %get-tuple-element.8), calls=%async_computation | async-start | bytes 6291456 | tf_op jit(solution)/shard_map/all_to_all | solution.py:354
  16.7 7.5 %collective-permute-start = (s32[16,128]{1,0:T(8,128)}, s32[16,128]{1,0:T(8,128)S(1)}, u32[]{:S(2)}, u32[]{:S(2)}) collective-permute-start(s32[16,128]{1,0:T(8,128)} %pair_tables.1), channel_id=1, source_target_pairs={{0,32},{32,0},{64,96},{96,64},{128,160},{160,128},{192,224},{224,1... | collective-permute-start | bytes 24584 | tf_op jit(solution)/shard_map/ppermute | solution.py:111

commit v8 on v7

--- a/solution.py
+++ b/solution.py
@@ -10,7 +10,6 @@
 
 GROUP = 16
 NONE = 16
-CHUNKS = 8
 LOADS = 4
 KINDS = 3
 PAIR_ROWS = 8
@@ -197,22 +196,21 @@
     )(counts, queries, keys, values)
 
 
-def unpack_kernel(order, heads, out, staged, sems):
-    peers, heads_here, rows, head_dim = heads.shape
-    step = rows // CHUNKS
-    copies = []
-    for chunk in range(CHUNKS):
-        span = pl.ds(chunk * step, step)
-        for peer in range(peers):
-            for j in range(heads_here):
-                head = order[0, place_to_slot(peer, j, heads_here)]
-                column = pl.multiple_of(head * head_dim, head_dim)
-                staged[span, pl.ds(column, head_dim)] = heads[peer, j, span, :]
-        copy = pltpu.make_async_copy(staged.at[span, :], out.at[span, :], sems.at[chunk])
-        copy.start()
-        copies.append(copy)
-    for copy in copies:
-        copy.wait()
+def static_slot(peer, j, heads_here):
+    chip, core = divmod(peer, CORES)
+    return chip * CORES * heads_here + j * CORES + (core if j % 2 == 0 else CORES - 1 - core)
+
+
+def unpack_kernel(order, heads, out, sem):
+    peers, heads_here, _, head_dim = heads.shape
+    held_order = order[...]
+    for peer in range(peers):
+        for j in range(heads_here):
+            slot = static_slot(peer, j, heads_here)
+            head = held_order[0, slot]
+            column = pl.multiple_of(head * head_dim, head_dim)
+            pltpu.make_async_copy(heads.at[peer, j], out.at[:, pl.ds(column, head_dim)], sem).start()
+    pltpu.make_async_copy(out, out, sem).wait()
 
 
 def unpack(order, heads):
@@ -221,11 +219,10 @@
     return pl.pallas_call(
         unpack_kernel,
         out_shape=jax.ShapeDtypeStruct((rows, columns), heads.dtype),
-        in_specs=[SMEM, VMEM],
+        in_specs=[VMEM, VMEM],
         out_specs=ANY,
         scratch_shapes=[
-            pltpu.VMEM((rows, columns), heads.dtype),
-            pltpu.SemaphoreType.DMA((CHUNKS,)),
+            pltpu.SemaphoreType.DMA,
         ],
         compiler_params=pltpu.CompilerParams(vmem_limit_bytes=8 * 1024 * 1024),
         name="unpack",

time: 128 us -> 128 us (level)
  no operation moved by 1% of the time
where the time goes in v8:
time: 128 us; the launch traced here: 127 us
  waiting for transfers between devices  60.9 us (48%)
  blocking collectives  34.9 us (27%)
  starting transfers between devices  13.8 us (11%)
  Pallas kernels  11.3 us (9%)
  between operations  4.89 us (4%)
    all_to_all x1, waiting for transfers between devices, on_device(): lax.all_to_all(packed, 'seq', split_axis=0, concat_axis=0, tiled=True)  60.9 us
    all_to_all x1, blocking collectives, on_device(): lax.all_to_all(attended, 'seq', split_axis=0, concat_axis=0, tiled=True)  34.9 us
    all_to_all x1, starting transfers between devices, on_device(): lax.all_to_all(packed, 'seq', split_axis=0, concat_axis=0, tiled=True)  11.8 us
    pallas_call x1, Pallas kernels, attend(): pl.pallas_call(functools.partial(heads_kernel, factor), out_shape=jax.Sha...  5.47 us
    pallas_call x1, Pallas kernels, pack(): pl.pallas_call(pack_kernel, out_shape=(jax.ShapeDtypeStruct((peers, heads...  2.9 us
  transfers between devices with their start and end apart: 2, of which 1 were waited for; matrix products, arithmetic and copies ran while one was open for 1% of the time, Pallas kernels for 1%

profile of v8, /device:TPU:1, one launch (start us, length us, event | category | flops | bytes accessed | tf_op | source)
XLA Modules:
  0.0 127.2 jit_solution(13702691871717971579)
XLA Ops:
  0.0 2.9 %pack.1 = (bf16[16,768,128]{2,1,0:T(8,128)(2,1)}, s32[1,128]{1,0:T(1,128)}) custom-call(s32[32]{0:T(128)} %counts.1, bf16[128,4096]{1,0:T(8,128)(2,1)} %queries.1, bf16[128,4096]{1,0:T(8,128)(2,1)} %keys.1, bf16[128,4096]{1,0:T(8,128)(2,1)} %values.1), custom_call_target="tpu_custom_call" | custom-call | tf_op jit(solution)/shard_map/pack/pallas_call | solution.py:177
  2.9 0.0 copy-start
  2.9 11.8 %all-to-all-start = ((bf16[16,768,128]{2,1,0:T(8,128)(2,1)}), bf16[16,768,128]{2,1,0:T(8,128)(2,1)S(1)}, u32[]{:S(2)}, u32[]{:S(2)}) async-start(bf16[16,768,128]{2,1,0:T(8,128)(2,1)} %get-tuple-element.8), calls=%async_computation | async-start | bytes 6291456 | tf_op jit(solution)/shard_map/all_to_all | solution.py:351
  14.8 1.9 %pair_tables.1 = s32[16,128]{1,0:T(8,128)} custom-call(s32[1]{0:T(128)} %bitcast.me, s32[32]{0:T(128)} %counts.1, s32[1,128]{1,0:T(1,128)} %get-tuple-element.7.order, s32[2,96]{1,0:T(2,128)} %lists.1), custom_call_target="tpu_custom_call" | custom-call | tf_op jit(solution)/shard_map/pair_tables/pallas_call | solution.py:102
  16.7 2.0 %collective-permute-start = (s32[16,128]{1,0:T(8,128)}, s32[16,128]{1,0:T(8,128)S(1)}, u32[]{:S(2)}, u32[]{:S(2)}) collective-permute-start(s32[16,128]{1,0:T(8,128)} %pair_tables.1), channel_id=1, source_target_pairs={{0,32},{32,0},{64,96},{96,64},{128,160},{160,128},{192,224},{224,1... | collective-permute-start | bytes 24584 | tf_op jit(solution)/shard_map/ppermute | solution.py:110
  18.7 0.0 copy-done
  18.7 0.6 constant_dynamic-slice_fusion.1
  24.1 0.0 collective-permute-done
  24.1 0.7 add_bitcast_fusion
  24.9 60.9 %all-to-all-done.parcels = bf16[16,768,128]{2,1,0:T(8,128)(2,1)S(1)} async-done(((bf16[16,768,128]{2,1,0:T(8,128)(2,1)}), bf16[16,768,128]{2,1,0:T(8,128)(2,1)S(1)}, u32[]{:S(2)}, u32[]{:S(2)}) %all-to-all-start) | async-done | bytes 3145760 | tf_op jit(solution)/shard_map/all_to_all | solution.py:351
  85.7 5.5 %attend.1 = bf16[16,2,128,128]{3,2,1,0:T(8,128)(2,1)S(1)} custom-call(s32[16,128]{1,0:T(8,128)S(1)} %pad_add_fusion.tables_in, bf16[16,768,128]{2,1,0:T(8,128)(2,1)S(1)} %all-to-all-done.parcels), custom_call_target="tpu_custom_call" | custom-call | tf_op jit(solution)/shard_map/attend/pallas_call | solution.py:327
  91.2 34.9 %all_to_all.10.heads = bf16[16,2,128,128]{3,2,1,0:T(8,128)(2,1)S(1)} all-to-all(bf16[16,2,128,128]{3,2,1,0:T(8,128)(2,1)S(1)} %attend.1), channel_id=1, replica_groups=mesh['seq'=16,'batch'=32] {'seq'}, dimensions={0} | all-to-all | bytes 2097152 | tf_op jit(solution)/shard_map/all_to_all | solution.py:354
  126.1 1.0 unpack.1
  (2 shorter events, 0.0 us)
Async XLA Ops:
  2.9 15.8 %copy-start = (s32[1,128]{1,0:T(1,128)S(1)}, s32[1,128]{1,0:T(1,128)}, u32[]{:S(2)}) copy-start(s32[1,128]{1,0:T(1,128)} %get-tuple-element.7.order) | copy-start | bytes 1540
  2.9 82.8 %all-to-all-start = ((bf16[16,768,128]{2,1,0:T(8,128)(2,1)}), bf16[16,768,128]{2,1,0:T(8,128)(2,1)S(1)}, u32[]{:S(2)}, u32[]{:S(2)}) async-start(bf16[16,768,128]{2,1,0:T(8,128)(2,1)} %get-tuple-element.8), calls=%async_computation | async-start | bytes 6291456 | tf_op jit(solution)/shard_map/all_to_all | solution.py:351
  16.7 7.5 %collective-permute-start = (s32[16,128]{1,0:T(8,128)}, s32[16,128]{1,0:T(8,128)S(1)}, u32[]{:S(2)}, u32[]{:S(2)}) collective-permute-start(s32[16,128]{1,0:T(8,128)} %pair_tables.1), channel_id=1, source_target_pairs={{0,32},{32,0},{64,96},{96,64},{128,160},{160,128},{192,224},{224,1... | collective-permute-start | bytes 24584 | tf_op jit(solution)/shard_map/ppermute | solution.py:110
